TPU v7x, 128 devices: a whole 4x4x4 slice. The times are simulated.
128 devices in a mesh: by: 16 (over z, x), bx: 8 (over y, core).
Axes of the slice: x: 4, y: 4, z: 4, core: 2. Of those that a mesh axis runs over, the one named last changes fastest.
Arguments:
- features: bfloat16 [512, 128, 256], P(('by', 'bx')), may hold values from -36 to 36
- depth_weight: float32 [512, 64, 128], P(('by', 'bx')), may hold values from 0.05 to 20
- depth_slot: int32 [512, 64, 128], P(('by', 'bx')), may hold values from 0 to 1023
- patch_count: int32 [512], P(('by', 'bx')), may hold values from 1 to 128, 49152 in all
- depth_first: int32 [512], P(('by', 'bx')), may hold values from 0 to 31
- depth_count: int32 [512], P(('by', 'bx')), may hold values from 16 to 32
- tile_dest: int32 [512, 32], P(('by', 'bx')), may hold values from 0 to 127, all different within a row; in each aligned block of 4 rows (0 to 3, 4 to 7, ...) at most 2 rows name the same one
- tile_cells: int32 [512, 1024], P(('by', 'bx')), may hold values from 0 to 1599
- conv_first: bfloat16 [3, 3, 256, 256], replicated, may hold values from -0.125 to 0.125
- conv_second: bfloat16 [3, 3, 256, 256], replicated, may hold values from -0.125 to 0.125
- grad_out: bfloat16 [640, 320, 256], P('by', 'bx'), may hold values from -6 to 6
Outputs:
- out_bev: bfloat16 [640, 320, 256], P('by', 'bx')
- grad_features: bfloat16 [512, 128, 256], P(('by', 'bx'))
- grad_depth_weight: float32 [512, 64, 128], P(('by', 'bx'))
- grad_conv_first: float32 [3, 3, 256, 256], replicated
- grad_conv_second: float32 [3, 3, 256, 256], replicated
Inputs may be any that keep to these rules, and one draw needn't show every extreme that they name: `tile_dest`: tile t is the device of index t along by+bx, by the slower; each block names 32 different tiles; the 4 blocks of one device name one tile at most 2 times, a bound that some device reaches. `tile_cells`: cell index inside a tile, row-major over 40 x 40. `depth_slot`: slot s lies in cell list s // 32 of its block. `patch_count`: all blocks together hold 512 * 128 * 3 // 4 live patches; some block is full.
All inputs are finite; a program needn't handle non-finite values.
Results may differ from a plain program's by a relative error of at most 0.0074.
Values may be sent and summed in bfloat16 or wider, within the bound.
No kernel may reach another device: no remote copies, remote signals or barrier semaphores. Data moves between devices by JAX's collectives and lax.ppermute only.
A program may use at most 128 MiB of HBM per device.

v0:
```python
from functools import partial

import jax
import jax.numpy as jnp
from jax import lax
from jax.experimental import pallas as pl
from jax.experimental.pallas import tpu as pltpu
from jax.sharding import PartitionSpec as P

CAP = 2
BINS = 64
LIVE = 128
SLOTS = 1024
LIST = 32
LISTS = 32
BLOCKS = 4
CH = 256
TILE = 40
CELLS = TILE * TILE
PITCH = 48
LEAD = 16
FLAT = 2160
WIDE0, WIDE = 48, 2048
CORE0, CORE = 112, 1920
F32 = jnp.float32
BF16 = jnp.bfloat16
VMEM = pl.BlockSpec(memory_space=pltpu.VMEM)
SMEM = pl.BlockSpec(memory_space=pltpu.SMEM)
PARAMS = pltpu.CompilerParams(vmem_limit_bytes=56 * 1024 * 1024)


def call(kernel, ins, out_shape, out_specs, scratch, flops, moved):
    return pl.pallas_call(
        kernel,
        in_specs=ins,
        out_shape=out_shape,
        out_specs=out_specs,
        scratch_shapes=scratch,
        compiler_params=PARAMS,
        cost_estimate=pl.CostEstimate(flops=flops, bytes_accessed=moved, transcendentals=0),
    )


def depth_parts(first_ref, count_ref, weight_ref, b):
    bins = lax.broadcasted_iota(jnp.int32, (BINS, LIVE), 0)
    first = first_ref[b]
    in_range = (bins >= first) & (bins < first + count_ref[b])
    live = jnp.where(in_range, weight_ref[b], 0.0)
    total = jnp.sum(live, axis=0, keepdims=True)
    return in_range, live / total, total


def masked_features(live_ref, feat_ref, b):
    patch = lax.broadcasted_iota(jnp.int32, (LIVE, CH), 0)
    return jnp.where(patch < live_ref[b], feat_ref[b].astype(F32), 0.0).astype(BF16)


def lift_kernel(
    first_ref,
    count_ref,
    live_ref,
    route_ref,
    feat_ref,
    weight_ref,
    slot_ref,
    out_ref,
    table_ref,
    prob,
    part,
):
    def wipe(i, c):
        out_ref[pl.ds(pl.multiple_of(i * 256, 256), 256), :] = jnp.zeros((256, CH), BF16)
        return c

    lax.fori_loop(0, 32, wipe, 0)
    low = lax.broadcasted_iota(jnp.int32, (8, LIVE), 0)

    def block(b, c):
        _, share, _ = depth_parts(first_ref, count_ref, weight_ref, b)
        prob[...] = share
        first = first_ref[b]
        pairs = (count_ref[b] + 1) // 2
        for chunk in range(4):

            def pair(i, acc):
                for step in range(2):
                    d = first + 2 * i + step
                    slot = jnp.broadcast_to(slot_ref[b, pl.ds(d, 1), :], (8, LIVE))
                    share = jnp.broadcast_to(prob[pl.ds(d, 1), :], (8, LIVE))
                    mine = jnp.where((slot & 7) == low, share, 0.0)
                    high = (slot >> 3) - chunk * 32
                    acc = [a + jnp.where(high == r, mine, 0.0) for r, a in enumerate(acc)]
                return acc

            acc = lax.fori_loop(0, pairs, pair, [jnp.zeros((8, LIVE), F32)] * 32)
            table_ref[b, chunk * 256 : (chunk + 1) * 256, :] = jnp.concatenate(acc, axis=0).astype(
                BF16
            )
        part[...] = jnp.dot(
            table_ref[b], masked_features(live_ref, feat_ref, b), preferred_element_type=F32
        ).astype(BF16)
        for k in range(LISTS):
            to = pl.multiple_of(route_ref[b * LISTS + k] * LIST, LIST)
            out_ref[pl.ds(to, LIST), :] = part[k * LIST : (k + 1) * LIST, :]
        return c

    lax.fori_loop(0, BLOCKS, block, 0)


def lift(first, count, live, route, features, weights, slots):
    return call(
        lift_kernel,
        [SMEM] * 4 + [VMEM] * 3,
        (
            jax.ShapeDtypeStruct((128 * CAP * LIST, CH), BF16),
            jax.ShapeDtypeStruct((BLOCKS, SLOTS, LIVE), BF16),
        ),
        (VMEM, VMEM),
        [pltpu.VMEM((BINS, LIVE), F32), pltpu.VMEM((SLOTS, CH), BF16)],
        300_000_000,
        6_000_000,
    )(first, count, live, route, features, weights, slots)


def pack_kernel(dest_ref, cell_ref, out_ref, route_ref, seen):
    def clear(i, c):
        seen[i] = 0
        return c

    lax.fori_loop(0, 128, clear, 0, unroll=8)
    out_ref[...] = jnp.full_like(out_ref, -1)
    for i in range(BLOCKS * LISTS):
        b, k = i // LISTS, i % LISTS
        tile = dest_ref[b, k]
        rank = seen[tile]
        seen[tile] = rank + 1
        to = tile * CAP + rank
        route_ref[i] = to
        out_ref[pl.ds(to, 1), :] = cell_ref[b : b + 1, k * LIST : (k + 1) * LIST]


def packed_cells(dest, cells):
    return call(
        pack_kernel,
        [SMEM, VMEM],
        (
            jax.ShapeDtypeStruct((128 * CAP, LIST), jnp.int32),
            jax.ShapeDtypeStruct((BLOCKS * LISTS,), jnp.int32),
        ),
        (VMEM, SMEM),
        [pltpu.SMEM((128,), jnp.int32)],
        1_000_000,
        100_000,
    )(dest, cells)


def splat_kernel(
    cell_ref, list_ref, gout_ref, base_ref, top_ref, bottom_ref, left_ref, right_ref, acc, hit, strip
):
    rows = 128
    span = 1024
    places = lax.broadcasted_iota(jnp.int32, (rows, span), 0).astype(F32).astype(BF16)
    one, zero = jnp.ones((), BF16), jnp.zeros((), BF16)
    for chunk in range(8):
        cells = cell_ref[chunk : chunk + 1, :]
        low = jnp.broadcast_to((cells & 127).astype(F32), (rows, span)).astype(BF16)
        high = jnp.broadcast_to((cells >> 7).astype(F32), (rows, span)).astype(BF16)
        same = jnp.where(low == places, one, zero)
        for m in range(13):
            end = min(rows, CELLS - m * rows)
            hit[m * rows : m * rows + end, :] = jnp.where(
                high == jnp.full((), m, BF16), same, zero
            )[:end, :]
        part = jnp.dot(
            hit[...], list_ref[chunk * span : (chunk + 1) * span, :], preferred_element_type=F32
        )
        if chunk == 0:
            acc[...] = part
        else:
            acc[...] += part
    base_ref[...] = acc[...].astype(BF16)
    top_ref[:80, :] = acc[:80, :].astype(BF16)
    bottom_ref[:80, :] = acc[CELLS - 80 :, :].astype(BF16)
    for y in range(TILE):
        strip[0, 2 * y : 2 * y + 2, :] = acc[TILE * y : TILE * y + 2, :]
        strip[1, 2 * y : 2 * y + 2, :] = acc[TILE * y + 38 : TILE * y + 40, :]
    left_ref[:80, :] = strip[0].astype(BF16)
    right_ref[:80, :] = strip[1].astype(BF16)
    for n, ref in enumerate((top_ref, bottom_ref, left_ref, right_ref)):
        ref[80:, :] = gout_ref[n]


def splat(cells, lists, gout_edges):
    strip = jax.ShapeDtypeStruct((160, CH), BF16)
    return call(
        splat_kernel,
        [VMEM] * 3,
        (jax.ShapeDtypeStruct((CELLS, CH), BF16),) + (strip,) * 4,
        (VMEM,) * 5,
        [pltpu.VMEM((CELLS, CH), F32), pltpu.VMEM((CELLS, 1024), BF16), pltpu.VMEM((2, 80, CH), F32)],
        6_700_000_000,
        6_000_000,
    )(cells, lists, gout_edges)


def corner_kernel(top_ref, bottom_ref, left_ref, right_ref, up_ref, down_ref):
    for strip_ref, out_ref, at in ((top_ref, up_ref, 0), (bottom_ref, down_ref, 76)):
        for n in range(2):
            out_ref[96 * n : 96 * n + 80, :] = strip_ref[80 * n : 80 * n + 80, :]
            left = left_ref[80 * n : 80 * n + 80, :].astype(F32)[at : at + 4, :]
            right = right_ref[80 * n : 80 * n + 80, :].astype(F32)[at : at + 4, :]
            out_ref[96 * n + 80 : 96 * n + 96, :] = jnp.concatenate(
                [left, right, jnp.zeros((8, CH), F32)], axis=0
            ).astype(BF16)


def with_corners(top, bottom, left, right):
    strip = jax.ShapeDtypeStruct((192, CH), BF16)
    return call(
        corner_kernel, [VMEM] * 4, (strip, strip), (VMEM, VMEM), [], 1_000_000, 600_000
    )(top, bottom, left, right)


def shifted(values, axis, step):
    count = lax.axis_size(axis)
    return lax.ppermute(
        values, axis, [(i, i + step) for i in range(count) if 0 <= i + step < count]
    )


def lay_out(flat, center, above_ref, below_ref, left_ref, right_ref, n):
    above = above_ref[96 * n : 96 * n + 96, :].astype(F32)
    below = below_ref[96 * n : 96 * n + 96, :].astype(F32)
    left = left_ref[80 * n : 80 * n + 80, :].astype(F32)
    right = right_ref[80 * n : 80 * n + 80, :].astype(F32)
    flat[...] = jnp.zeros_like(flat)

    def spot(y, x):
        return 8 + (y + 2) * PITCH + LEAD + x

    for y in range(TILE):
        flat[spot(y, 0) : spot(y, 0) + TILE, :] = center[y * TILE : (y + 1) * TILE, :].astype(F32)
        flat[spot(y, -2) : spot(y, 0), :] = left[2 * y : 2 * y + 2, :]
        flat[spot(y, 40) : spot(y, 42), :] = right[2 * y : 2 * y + 2, :]
    for r in range(2):
        for rows, y in ((above, r - 2), (below, 40 + r)):
            flat[spot(y, 0) : spot(y, 40), :] = rows[r * TILE : (r + 1) * TILE, :]
            flat[spot(y, -2) : spot(y, 0), :] = rows[80 + 2 * r : 82 + 2 * r, :]
            flat[spot(y, 40) : spot(y, 42), :] = rows[84 + 2 * r : 86 + 2 * r, :]


def spread(flat, wide):
    step = 144
    for at in range(0, FLAT, step):
        for j in range(3):
            wide[at : at + step, j * CH : (j + 1) * CH] = flat[at + 7 + j : at + 7 + j + step, :].astype(
                BF16
            )


def taps(wide, weights, start, rows):
    total = None
    for i in range(3):
        at = pl.multiple_of(start + (i - 1) * PITCH, 16)
        part = jnp.dot(
            wide[pl.ds(at, rows), :],
            weights[i * 3 * CH : (i + 1) * 3 * CH, :],
            preferred_element_type=F32,
        )
        total = part if total is None else total + part
    return total


def flip_kernel(first_ref, second_ref, one_ref, two_ref):
    for source, out in ((first_ref, one_ref), (second_ref, two_ref)):
        for tap in range(9):
            taken = source[(8 - tap) * CH : (9 - tap) * CH, :].astype(F32)
            out[tap * CH : (tap + 1) * CH, :] = taken.T.astype(BF16)


def flipped(first, second):
    out = jax.ShapeDtypeStruct((9 * CH, CH), BF16)
    return call(
        flip_kernel, [VMEM] * 2, (out, out), (VMEM, VMEM), [], 10_000_000, 5_000_000
    )(first, second)


def place_mask(by, bx, start, rows, rim):
    n = lax.broadcasted_iota(jnp.int32, (rows, 128), 0) + (start - LEAD + 1)
    line = (n * 87382) >> 22
    x = n - line * PITCH - 1
    y = line - 2
    near = (y >= -rim) & (y < TILE + rim) & (x >= -rim) & (x < TILE + rim)
    gy, gx = y + by * TILE, x + bx * TILE
    inside = near & (gy >= 0) & (gy < 16 * TILE) & (gx >= 0) & (gx < 8 * TILE)
    return jnp.concatenate([jnp.where(inside, 1.0, 0.0)] * 2, axis=1) > 0.5


def kernel_sums(wide, turned, out):
    for tap in range(9):
        i, j = tap // 3, tap % 3
        at = WIDE0 + (i - 1) * PITCH
        got = jnp.dot(
            turned[...], wide[at : at + WIDE, j * CH : (j + 1) * CH], preferred_element_type=F32
        ).T.astype(BF16)
        for h in range(2):
            to = (2 * tap + h) * CH
            out[to : to + CH, :] = got[:, h * 128 : (h + 1) * 128]


def turn(spot_ref, wide, turned):
    for k in range(WIDE // 256):
        at = WIDE0 + k * 256
        inside = place_mask(spot_ref[0], spot_ref[1], at, 256, 0)
        values = wide[at : at + 256, CH : 2 * CH].astype(F32)
        turned[:, k * 256 : (k + 1) * 256] = jnp.where(inside, values, 0.0).T.astype(BF16)


def act_kernel(
    spot_ref,
    first_ref,
    second_ref,
    base_ref,
    gout_ref,
    above_ref,
    below_ref,
    left_ref,
    right_ref,
    hidden_ref,
    fcot_ref,
    sums_ref,
    wide,
    gwide,
    flat,
    flat2,
    turned,
):
    rims = (above_ref, below_ref, left_ref, right_ref)
    lay_out(flat, base_ref, *rims, 0)
    spread(flat, wide)
    lay_out(flat2, gout_ref, *rims, 1)
    spread(flat2, gwide)
    flat[...] = jnp.zeros_like(flat)
    flat2[...] = jnp.zeros_like(flat2)

    def activate(k, c):
        at = pl.multiple_of(WIDE0 + k * 512, 16)
        first_act = taps(wide, first_ref, at, 512)
        hidden_cot = taps(gwide, second_ref, at, 512)
        inside = place_mask(spot_ref[0], spot_ref[1], at, 512, 1)
        sig = jax.nn.sigmoid(first_act)
        to = pl.ds(pl.multiple_of(at + 8, 8), 512)
        flat2[to, :] = jnp.where(inside, first_act * sig, 0.0)
        slope = sig * (1.0 + first_act * (1.0 - sig))
        flat[to, :] = jnp.where(inside, hidden_cot * slope, 0.0)
        return c

    lax.fori_loop(0, WIDE // 512, activate, 0)
    spread(flat, fcot_ref)
    turn(spot_ref, fcot_ref, turned)
    kernel_sums(wide, turned, sums_ref.at[0])
    spread(flat2, hidden_ref)
    turn(spot_ref, gwide, turned)
    kernel_sums(hidden_ref, turned, sums_ref.at[1])


def activate_tile(spot, first, second, base, gout, rims):
    wide = jax.ShapeDtypeStruct((FLAT, 3 * CH), BF16)
    return call(
        act_kernel,
        [SMEM] + [VMEM] * 8,
        (wide, wide, jax.ShapeDtypeStruct((2, 18 * CH, 128), BF16)),
        (VMEM,) * 3,
        [
            pltpu.VMEM((FLAT, 3 * CH), BF16),
            pltpu.VMEM((FLAT, 3 * CH), BF16),
            pltpu.VMEM((FLAT + 16, CH), F32),
            pltpu.VMEM((FLAT + 16, CH), F32),
            pltpu.VMEM((CH, WIDE), BF16),
        ],
        9_000_000_000,
        16_000_000,
    )(spot, first, second, base, gout, *rims)


def strip_pads(got, out, k):
    for r in range(5):
        lines = [got[(2 * r + s) * PITCH : (2 * r + s) * PITCH + TILE, :] for s in range(2)]
        to = pl.multiple_of(k * 400 + r * 80, 16)
        out[pl.ds(to, 80), :] = jnp.concatenate(lines, axis=0).astype(BF16)


def back_kernel(first_ref, cell_ref, fcot_ref, out_ref, tile):
    def back(k, c):
        at = pl.multiple_of(CORE0 + k * 480, 16)
        strip_pads(taps(fcot_ref, first_ref, at, 480), tile, k)
        return c

    lax.fori_loop(0, 4, back, 0)
    tile[CELLS:, :] = jnp.zeros((1664 - CELLS, CH), BF16)
    places = lax.broadcasted_iota(jnp.int32, (512, 128), 1).astype(F32).astype(BF16)
    one, zero = jnp.ones((), BF16), jnp.zeros((), BF16)

    def pick(k, c):
        at = pl.multiple_of(k * 512, 512)
        cells = jnp.broadcast_to(cell_ref[pl.ds(at, 512), :], (512, 128))
        high = (cells >> 7).astype(F32).astype(BF16)
        same = jnp.where((cells & 127).astype(F32).astype(BF16) == places, one, zero)
        hits = [jnp.where(high == jnp.full((), m, BF16), same, zero) for m in range(13)]
        out_ref[pl.ds(at, 512), :] = jnp.dot(
            jnp.concatenate(hits, axis=1), tile[...], preferred_element_type=F32
        ).astype(BF16)
        return c

    lax.fori_loop(0, 16, pick, 0)


def send_back(first, cells, fcot_wide):
    return call(
        back_kernel,
        [VMEM] * 3,
        jax.ShapeDtypeStruct((128 * CAP * LIST, CH), BF16),
        VMEM,
        [pltpu.VMEM((1664, CH), BF16)],
        9_000_000_000,
        12_000_000,
    )(first, cells, fcot_wide)


def out_kernel(second_ref, hidden_ref, out_ref):
    def forward(k, c):
        at = pl.multiple_of(CORE0 + k * 480, 16)
        strip_pads(taps(hidden_ref, second_ref, at, 480), out_ref, k)
        return c

    lax.fori_loop(0, 4, forward, 0)


def outward(second, hidden_wide):
    return call(
        out_kernel,
        [VMEM] * 2,
        jax.ShapeDtypeStruct((CELLS, CH), BF16),
        VMEM,
        [],
        2_300_000_000,
        5_000_000,
    )(second, hidden_wide)


def widen_kernel(sums_ref, one_ref, two_ref):
    for by in range(16):
        for bx in range(8):
            values = sums_ref[bx, by].astype(F32)
            at = (by * 8 + bx) * 72
            done = 0
            while done < 72:
                part, row = divmod(at + done, CH)
                n, part = divmod(part, 18)
                size = min(72 - done, CH - row)
                out = (one_ref, two_ref)[n]
                lanes = slice(part % 2 * 128, part % 2 * 128 + 128)
                out[part // 2, row : row + size, lanes] = values[done : done + size, :]
                done += size


def widen(sums):
    out = jax.ShapeDtypeStruct((9, CH, CH), F32)
    return call(widen_kernel, [VMEM], (out, out), (VMEM, VMEM), [], 1_000_000, 7_000_000)(sums)


def settle_kernel(first_ref, count_ref, live_ref, route_ref, feat_ref, weight_ref, slot_ref, table_ref, back_ref, gfeat_ref, gweight_ref, part, cot, pick):
    for b in range(BLOCKS):
        for k in range(LISTS):
            at = pl.multiple_of(route_ref[b * LISTS + k] * LIST, LIST)
            part[k * LIST : (k + 1) * LIST, :] = back_ref[pl.ds(at, LIST), :]
        masked = masked_features(live_ref, feat_ref, b)
        cot[...] = lax.dot_general(
            part[...], masked, (((1,), (1,)), ((), ())), preferred_element_type=F32
        )
        got = jnp.dot(table_ref[b], part[...], preferred_element_type=F32)
        patch = lax.broadcasted_iota(jnp.int32, (LIVE, CH), 0)
        gfeat_ref[b] = jnp.where(patch < live_ref[b], got, 0.0).astype(BF16)
        pick[...] = jnp.zeros_like(pick)
        first = first_ref[b]

        def eight(q, c):
            at = pl.multiple_of(q * 8, 8)
            slot = slot_ref[b, pl.ds(at, 8), :]
            low, high = slot & 7, slot >> 3

            def group(g, acc):
                for r in range(16):
                    row = g * 16 + r
                    rows = cot[pl.ds(pl.multiple_of(row * 8, 8), 8), :]
                    found = jnp.take_along_axis(rows, low, axis=0, mode="promise_in_bounds")
                    acc = jnp.where(high == row, found, acc)
                return acc

            pick[pl.ds(at, 8), :] = lax.fori_loop(0, 8, group, jnp.zeros((8, LIVE), F32))
            return c

        lax.fori_loop(first >> 3, (first + count_ref[b] + 7) >> 3, eight, 0)
        in_range, prob, total = depth_parts(first_ref, count_ref, weight_ref, b)
        picked = pick[...]
        mean = jnp.sum(prob * picked, axis=0, keepdims=True)
        gweight_ref[b] = jnp.where(in_range, (picked - mean) / total, 0.0)


def settle(first, count, live, route, features, weights, slots, table, back):
    return call(
        settle_kernel,
        [SMEM] * 4 + [VMEM] * 5,
        (
            jax.ShapeDtypeStruct((BLOCKS, LIVE, CH), BF16),
            jax.ShapeDtypeStruct((BLOCKS, BINS, LIVE), F32),
        ),
        (VMEM, VMEM),
        [
            pltpu.VMEM((SLOTS, CH), BF16),
            pltpu.VMEM((SLOTS, LIVE), F32),
            pltpu.VMEM((BINS, LIVE), F32),
        ],
        600_000_000,
        8_000_000,
    )(first, count, live, route, features, weights, slots, table, back)


def exchanged(values):
    return lax.all_to_all(values, ("by", "bx"), split_axis=0, concat_axis=0, tiled=True)


def on_device(
    features,
    depth_weight,
    depth_slot,
    patch_count,
    depth_first,
    depth_count,
    tile_dest,
    tile_cells,
    conv_first,
    conv_second,
    grad_out,
):
    by, bx = lax.axis_index("by"), lax.axis_index("bx")
    me = by * lax.axis_size("bx") + bx
    devices = lax.axis_size("by") * lax.axis_size("bx")
    spot = jnp.stack([by, bx]).astype(jnp.int32)
    groups = BLOCKS * LISTS
    first_taps = conv_first.reshape(9 * CH, CH)
    second_taps = conv_second.reshape(9 * CH, CH)

    cells, route = packed_cells(tile_dest, tile_cells)
    cells = exchanged(cells.reshape(devices, CAP, LIST)).reshape(devices * CAP * LIST)
    cell_column = cells.reshape(-1, 1)
    outgoing, table = lift(
        depth_first, depth_count, patch_count, route, features, depth_weight, depth_slot
    )
    arrived = exchanged(outgoing)

    _, edge = lax.optimization_barrier((outgoing, grad_out))
    gout_edges = jnp.stack(
        [
            edge[:2].reshape(80, CH),
            edge[38:].reshape(80, CH),
            edge[:, :2].reshape(80, CH),
            edge[:, 38:].reshape(80, CH),
        ]
    )
    turned_table = jnp.swapaxes(table, 1, 2)
    _, first_late, second_late = lax.optimization_barrier((outgoing, first_taps, second_taps))
    first_flip, second_flip = flipped(first_late, second_late)
    arrived, cell_column, turned_table, first_flip, second_flip = lax.optimization_barrier(
        (arrived, cell_column, turned_table, first_flip, second_flip)
    )

    base, top, bottom, left, right = splat(cells.reshape(8, 1024), arrived, gout_edges)
    from_left, from_right = shifted(right, "bx", 1), shifted(left, "bx", -1)
    up, down = with_corners(top, bottom, from_left, from_right)
    rims = (shifted(down, "by", 1), shifted(up, "by", -1), from_left, from_right)
    hidden_wide, fcot_wide, sums = activate_tile(
        spot, first_taps, second_flip, base, grad_out.reshape(CELLS, CH), rims
    )
    sums = exchanged(sums.reshape(devices, 72, 128))
    returning = send_back(first_flip, cell_column, fcot_wide)
    returning, sums = lax.optimization_barrier((returning, sums))
    sums = jnp.sum(sums.astype(F32), axis=0).astype(BF16)
    sums = lax.all_to_all(
        jnp.broadcast_to(sums, (16, 72, 128)), "by", split_axis=0, concat_axis=0, tiled=True
    )
    returning, sums = lax.optimization_barrier((returning, sums))
    sums = lax.all_gather(sums, "bx", axis=0)
    returned = exchanged(returning)
    out_bev = outward(second_taps, hidden_wide)
    returned, out_bev = lax.optimization_barrier((returned, out_bev))
    feature_grad, weight_grad = settle(
        depth_first,
        depth_count,
        patch_count,
        route,
        features,
        depth_weight,
        depth_slot,
        turned_table,
        returned,
    )
    sums, weight_grad = lax.optimization_barrier((sums, weight_grad))
    grad_first, grad_second = widen(sums)
    return (
        out_bev.reshape(TILE, TILE, CH),
        feature_grad,
        weight_grad,
        grad_first.reshape(3, 3, CH, CH),
        grad_second.reshape(3, 3, CH, CH),
    )


def solution(mesh):
    placed = (
        P(("by", "bx"), None, None),
        P(("by", "bx"), None, None),
        P(("by", "bx"), None, None),
        P(("by", "bx")),
        P(("by", "bx")),
        P(("by", "bx")),
        P(("by", "bx"), None),
        P(("by", "bx"), None),
        P(),
        P(),
        P("by", "bx", None),
    )
    return jax.shard_map(
        on_device,
        mesh=mesh,
        in_specs=placed,
        out_specs=(
            P("by", "bx", None),
            P(("by", "bx"), None, None),
            P(("by", "bx"), None, None),
            P(),
            P(),
        ),
        check_vma=False,
    )
```

profile of v0, /device:TPU:1, one launch (start us, length us, event | category | flops | bytes accessed | tf_op | source)
XLA Modules:
  0.0 284.7 jit_solution(14070485643201117762)
XLA Ops:
  7.2 2.1 shard_map.146
  9.3 11.5 %all-to-all-start.1 = ((s32[128,2,32]{2,1,0:T(2,128)}), s32[128,2,32]{2,1,0:T(2,128)S(1)}, u32[]{:S(2)}, u32[]{:S(2)}) async-start(s32[128,2,32]{2,1,0:T(2,128)} %bitcast.29), calls=%async_computation.1 | async-start | bytes 262144 | tf_op jit(solution)/shard_map/all_to_all | solution.py:530
  20.8 11.3 %shard_map.147 = (bf16[8192,256]{1,0:T(8,128)(2,1)}, bf16[4,1024,128]{2,1,0:T(8,128)(2,1)}) custom-call(s32[4]{0:T(128)} %first_ref.3, s32[4]{0:T(128)} %count_ref.3, s32[4]{0:T(128)} %live_ref.3, s32[128]{0:T(128)} %get-tuple-element.41.route_ref, bf16[4,128,256]{2,1,0:T(8,128)(2,1)} %feat_ref.3, f32[4,64,128]{2,1,0:T(8,128)} %weight_ref.3, ...), custom_call_target="tpu_custom_call" | custom-call | flops 300000000 | bytes 6000000 | tf_op jit(solution)/shard_map/pallas_call | solution.py:111
  32.0 11.5 %all-to-all-start = ((bf16[128,64,256]{2,1,0:T(8,128)(2,1)}), bf16[128,64,256]{2,1,0:T(8,128)(2,1)}, u32[]{:S(2)}, u32[]{:S(2)}) async-start(bf16[128,64,256]{2,1,0:T(8,128)(2,1)} %bitcast.18), calls=%async_computation | async-start | bytes 8388608 | tf_op jit(solution)/shard_map/all_to_all | solution.py:530
  46.0 3.4 %shard_map.148 = (bf16[2304,256]{1,0:T(8,128)(2,1)}, bf16[2304,256]{1,0:T(8,128)(2,1)}) custom-call(bf16[2304,256]{1,0:T(8,128)(2,1)} %bitcast.23, bf16[2304,256]{1,0:T(8,128)(2,1)} %bitcast.25), custom_call_target="tpu_custom_call" | custom-call | flops 10000000 | bytes 5000000 | tf_op jit(solution)/shard_map/pallas_call | solution.py:283
  51.9 44.5 %all-to-all-done = bf16[128,64,256]{2,1,0:T(8,128)(2,1)} async-done(((bf16[128,64,256]{2,1,0:T(8,128)(2,1)}), bf16[128,64,256]{2,1,0:T(8,128)(2,1)}, u32[]{:S(2)}, u32[]{:S(2)}) %all-to-all-start) | async-done | bytes 4194336 | tf_op jit(solution)/shard_map/all_to_all | solution.py:530
  96.4 10.6 %shard_map.149 = (bf16[1600,256]{1,0:T(8,128)(2,1)}, bf16[160,256]{1,0:T(8,128)(2,1)}, bf16[160,256]{1,0:T(8,128)(2,1)}, bf16[160,256]{1,0:T(8,128)(2,1)}, bf16[160,256]{1,0:T(8,128)(2,1)}) custom-call(s32[8,1024]{1,0:T(8,128)} %reshape_reshape.7.cell_ref, bf16[8192,256]{1,0:T(8,128)(2,1)} %bitcast.1.list_ref, bf16[4,80,256]{2,1,0:T(8,128)(2,1)} %pad_maximum_fusion.gout_ref), custom_call_target="tpu_custom_call" | custom-call | flops 6700000256 | bytes 6000000 | tf_op jit(solution)/shard_map/pallas_call | solution.py:195
  107.0 2.8 collective-permute-start
  109.8 1.9 collective-permute-start.1
  111.8 4.0 %collective-permute-done.1.right_ref = bf16[160,256]{1,0:T(8,128)(2,1)S(1)} collective-permute-done((bf16[160,256]{1,0:T(8,128)(2,1)}, bf16[160,256]{1,0:T(8,128)(2,1)S(1)}, u32[]{:S(2)}, u32[]{:S(2)}) %collective-permute-start.1) | collective-permute-done | bytes 81952 | tf_op jit(solution)/shard_map/ppermute | solution.py:226
  116.4 1.7 shard_map.150
  119.4 1.5 collective-permute-start.3
  121.5 3.4 %collective-permute-done.3.below_ref = bf16[192,256]{1,0:T(8,128)(2,1)S(1)} collective-permute-done((bf16[192,256]{1,0:T(8,128)(2,1)}, bf16[192,256]{1,0:T(8,128)(2,1)S(1)}, u32[]{:S(2)}, u32[]{:S(2)}) %collective-permute-start.3) | collective-permute-done | bytes 98336 | tf_op jit(solution)/shard_map/ppermute | solution.py:226
  125.6 21.1 %shard_map.151 = (bf16[2160,768]{1,0:T(8,128)(2,1)}, bf16[2160,768]{1,0:T(8,128)(2,1)}, bf16[2,4608,128]{2,1,0:T(8,128)(2,1)}) custom-call(s32[2]{0:T(128)} %pad_add_fusion.spot_ref, bf16[2304,256]{1,0:T(8,128)(2,1)} %bitcast.24, bf16[2304,256]{1,0:T(8,128)(2,1)} %get-tuple-element.51.second_ref, bf16[1600,256]{1,0:T(8,128)(2,1)} %get-tuple-element.54.base_ref, ...), custom_call_target="tpu_custom_call" | custom-call | flops 8999999488 | bytes 16000000 | tf_op jit(solution)/shard_map/pallas_call | solution.py:369
  146.7 10.0 %all-to-all-start.2 = ((bf16[128,72,128]{2,1,0:T(8,128)(2,1)}), bf16[128,72,128]{2,1,0:T(8,128)(2,1)S(1)}, u32[]{:S(2)}, u32[]{:S(2)}) async-start(bf16[128,72,128]{2,1,0:T(8,128)(2,1)} %bitcast.22), calls=%async_computation.2 | async-start | bytes 4718592 | tf_op jit(solution)/shard_map/all_to_all | solution.py:530
  156.7 2.7 copy.20.cell_ref
  159.5 19.5 %shard_map.152 = bf16[8192,256]{1,0:T(8,128)(2,1)} custom-call(bf16[2304,256]{1,0:T(8,128)(2,1)} %get-tuple-element.49.first_ref, s32[8192,1]{1,0:T(8,128)} %copy.20.cell_ref, bf16[2160,768]{1,0:T(8,128)(2,1)} %get-tuple-element.61.fcot_ref), custom_call_target="tpu_custom_call" | custom-call | flops 8999999488 | bytes 12000000 | tf_op jit(solution)/shard_map/pallas_call | solution.py:419
  179.0 11.0 %all-to-all-done.2 = bf16[128,72,128]{2,1,0:T(8,128)(2,1)S(1)} async-done(((bf16[128,72,128]{2,1,0:T(8,128)(2,1)}), bf16[128,72,128]{2,1,0:T(8,128)(2,1)S(1)}, u32[]{:S(2)}, u32[]{:S(2)}) %all-to-all-start.2) | async-done | bytes 2359328 | tf_op jit(solution)/shard_map/all_to_all | solution.py:530
  190.5 11.4 %all_to_all.39 = bf16[16,72,128]{2,1,0:T(8,128)(2,1)} all-to-all(bf16[16,72,128]{2,1,0:T(8,128)(2,1)S(1)} %broadcast_in_dim.3), channel_id=1, replica_groups=mesh['by'=16,'bx'=8] {'by'}, dimensions={0} | all-to-all | bytes 589824 | tf_op jit(solution)/shard_map/all_to_all | solution.py:589
  201.8 6.4 %all-to-all-start.4 = ((bf16[128,64,256]{2,1,0:T(8,128)(2,1)}), bf16[128,64,256]{2,1,0:T(8,128)(2,1)}, u32[]{:S(2)}, u32[]{:S(2)}) async-start(bf16[128,64,256]{2,1,0:T(8,128)(2,1)} %bitcast.19), calls=%async_computation.4 | async-start | bytes 8388608 | tf_op jit(solution)/shard_map/all_to_all | solution.py:530
  209.0 6.2 %shard_map.153 = bf16[1600,256]{1,0:T(8,128)(2,1)} custom-call(bf16[2304,256]{1,0:T(8,128)(2,1)} %bitcast.26, bf16[2160,768]{1,0:T(8,128)(2,1)} %get-tuple-element.66.hidden_ref), custom_call_target="tpu_custom_call" | custom-call | flops 2300000000 | bytes 5000000 | tf_op jit(solution)/shard_map/pallas_call | solution.py:440
  215.2 51.9 %all-to-all-done.4 = bf16[128,64,256]{2,1,0:T(8,128)(2,1)} async-done(((bf16[128,64,256]{2,1,0:T(8,128)(2,1)}), bf16[128,64,256]{2,1,0:T(8,128)(2,1)}, u32[]{:S(2)}, u32[]{:S(2)}) %all-to-all-start.4) | async-done | bytes 4194336 | tf_op jit(solution)/shard_map/all_to_all | solution.py:530
  267.0 6.8 %shard_map.154 = (bf16[4,128,256]{2,1,0:T(8,128)(2,1)}, f32[4,64,128]{2,1,0:T(8,128)}) custom-call(s32[4]{0:T(128)} %first_ref.3, s32[4]{0:T(128)} %count_ref.3, s32[4]{0:T(128)} %live_ref.3, s32[128]{0:T(128)} %get-tuple-element.41.route_ref, bf16[4,128,256]{2,1,0:T(8,128)(2,1)} %feat_ref.3, f32[4,64,128]{2,1,0:T(8,128)} %weight_ref.3, ...), custom_call_target="tpu_custom_call" | custom-call | flops 600000000 | bytes 8000000 | tf_op jit(solution)/shard_map/pallas_call | solution.py:511
  273.9 4.0 %shard_map.155 = (f32[9,256,256]{2,1,0:T(8,128)}, f32[9,256,256]{2,1,0:T(8,128)}) custom-call(bf16[8,16,72,128]{3,2,1,0:T(8,128)(2,1)} %bitcast.21), custom_call_target="tpu_custom_call" | custom-call | flops 1000000 | bytes 7000000 | tf_op jit(solution)/shard_map/pallas_call | solution.py:469
  (28 shorter events, 9.2 us)
Async XLA Ops:
  9.3 22.8 %all-to-all-start.1 = ((s32[128,2,32]{2,1,0:T(2,128)}), s32[128,2,32]{2,1,0:T(2,128)S(1)}, u32[]{:S(2)}, u32[]{:S(2)}) async-start(s32[128,2,32]{2,1,0:T(2,128)} %bitcast.29), calls=%async_computation.1 | async-start | bytes 262144 | tf_op jit(solution)/shard_map/all_to_all | solution.py:530
  32.0 11.5 %copy-start = (bf16[4,1024,128]{2,1,0:T(8,128)(2,1)S(1)}, bf16[4,1024,128]{2,1,0:T(8,128)(2,1)}, u32[]{:S(2)}) copy-start(bf16[4,1024,128]{2,1,0:T(8,128)(2,1)} %get-tuple-element.44) | copy-start | bytes 3145732
  32.0 64.3 %all-to-all-start = ((bf16[128,64,256]{2,1,0:T(8,128)(2,1)}), bf16[128,64,256]{2,1,0:T(8,128)(2,1)}, u32[]{:S(2)}, u32[]{:S(2)}) async-start(bf16[128,64,256]{2,1,0:T(8,128)(2,1)} %bitcast.18), calls=%async_computation | async-start | bytes 8388608 | tf_op jit(solution)/shard_map/all_to_all | solution.py:530
  107.0 4.8 %collective-permute-start = (bf16[160,256]{1,0:T(8,128)(2,1)}, bf16[160,256]{1,0:T(8,128)(2,1)S(1)}, u32[]{:S(2)}, u32[]{:S(2)}) collective-permute-start(bf16[160,256]{1,0:T(8,128)(2,1)} %get-tuple-element.57), channel_id=1, source_target_pairs={{0,1},{1,2},{2,3},{3,4},{4,5},{5,6},{6,7},{8,9},{9,10},{10,11},{11... | collective-permute-start | bytes 245768 | tf_op jit(solution)/shard_map/ppermute | solution.py:226
  109.8 6.0 %collective-permute-start.1 = (bf16[160,256]{1,0:T(8,128)(2,1)}, bf16[160,256]{1,0:T(8,128)(2,1)S(1)}, u32[]{:S(2)}, u32[]{:S(2)}) collective-permute-start(bf16[160,256]{1,0:T(8,128)(2,1)} %get-tuple-element.58), channel_id=1, source_target_pairs={{1,0},{2,1},{3,2},{4,3},{5,4},{6,5},{7,6},{9,8},{10,9},{11,10},{12... | collective-permute-start | bytes 245768 | tf_op jit(solution)/shard_map/ppermute | solution.py:226
  111.7 4.0 %copy-start.1 = (bf16[160,256]{1,0:T(8,128)(2,1)}, bf16[160,256]{1,0:T(8,128)(2,1)S(1)}, u32[]{:S(2)}) copy-start(bf16[160,256]{1,0:T(8,128)(2,1)S(1)} %collective-permute-done.left_ref) | copy-start | bytes 245764
  115.8 0.6 copy-start.2
  118.1 3.4 %collective-permute-start.2 = (bf16[192,256]{1,0:T(8,128)(2,1)}, bf16[192,256]{1,0:T(8,128)(2,1)S(1)}, u32[]{:S(2)}, u32[]{:S(2)}) collective-permute-start(bf16[192,256]{1,0:T(8,128)(2,1)} %get-tuple-element.59), channel_id=1, source_target_pairs={{0,8},{8,16},{16,24},{24,32},{32,40},{40,48},{48,56},{56,64},{64,7... | collective-permute-start | bytes 294920 | tf_op jit(solution)/shard_map/ppermute | solution.py:226
  119.4 5.6 %collective-permute-start.3 = (bf16[192,256]{1,0:T(8,128)(2,1)}, bf16[192,256]{1,0:T(8,128)(2,1)S(1)}, u32[]{:S(2)}, u32[]{:S(2)}) collective-permute-start(bf16[192,256]{1,0:T(8,128)(2,1)} %get-tuple-element.60), channel_id=1, source_target_pairs={{8,0},{16,8},{24,16},{32,24},{40,32},{48,40},{56,48},{64,56},{72,6... | collective-permute-start | bytes 294920 | tf_op jit(solution)/shard_map/ppermute | solution.py:226
  121.5 3.4 %copy-start.3 = (bf16[192,256]{1,0:T(8,128)(2,1)}, bf16[192,256]{1,0:T(8,128)(2,1)S(1)}, u32[]{:S(2)}) copy-start(bf16[192,256]{1,0:T(8,128)(2,1)S(1)} %collective-permute-done.2.above_ref) | copy-start | bytes 294916
  125.0 0.6 copy-start.4
  146.7 43.3 %all-to-all-start.2 = ((bf16[128,72,128]{2,1,0:T(8,128)(2,1)}), bf16[128,72,128]{2,1,0:T(8,128)(2,1)S(1)}, u32[]{:S(2)}, u32[]{:S(2)}) async-start(bf16[128,72,128]{2,1,0:T(8,128)(2,1)} %bitcast.22), calls=%async_computation.2 | async-start | bytes 4718592 | tf_op jit(solution)/shard_map/all_to_all | solution.py:530
  201.8 65.2 %all-to-all-start.4 = ((bf16[128,64,256]{2,1,0:T(8,128)(2,1)}), bf16[128,64,256]{2,1,0:T(8,128)(2,1)}, u32[]{:S(2)}, u32[]{:S(2)}) async-start(bf16[128,64,256]{2,1,0:T(8,128)(2,1)} %bitcast.19), calls=%async_computation.4 | async-start | bytes 8388608 | tf_op jit(solution)/shard_map/all_to_all | solution.py:530
  208.3 65.6 %all-gather.3.cloned.1.call-start = ((), (), s32[]{:S(2)}) async-start(), calls=%async_computation.5 | async-start | bytes 2654208 | tf_op jit(solution)/shard_map/all_gather | solution.py:593
Sparse Core Ops, SparseCore 0:
  210.8 56.5 all-gather.2
where the time goes:
time: 286 us; the launch traced here: 285 us
  waiting for transfers between devices  116 us (41%)
  Pallas kernels  86.7 us (30%)
  starting transfers between devices  47 us (16%)
  between operations  14.2 us (5%)
  blocking collectives  11.4 us (4%)
  local copies, waits for them, and re-layouts  8.21 us (3%)
    all_to_all x4, waiting for transfers between devices, exchanged(): lax.all_to_all(values, ('by', 'bx'), split_axis=0, concat_axis=0, tiled=T...  107 us
    all_to_all x4, starting transfers between devices, exchanged(): lax.all_to_all(values, ('by', 'bx'), split_axis=0, concat_axis=0, tiled=T...  39.5 us
    pallas_call x1, Pallas kernels, activate_tile(): call(act_kernel, [SMEM] + [VMEM] * 8, (wide, wide, jax.ShapeDtypeStruct((...  21.1 us
    pallas_call x1, Pallas kernels, send_back(): call(back_kernel, [VMEM] * 3, jax.ShapeDtypeStruct((128 * CAP * LIST, CH)...  19.5 us
    all_to_all x1, blocking collectives, on_device(): lax.all_to_all(jnp.broadcast_to(sums, (16, 72, 128)), 'by', split_axis=0,...  11.4 us
    pallas_call x1, Pallas kernels, lift(): call(lift_kernel, [SMEM] * 4 + [VMEM] * 3, (jax.ShapeDtypeStruct((128 * C...  11.3 us
    pallas_call x1, Pallas kernels, splat(): call(splat_kernel, [VMEM] * 3, (jax.ShapeDtypeStruct((CELLS, CH), BF16),)...  10.6 us
    ppermute x4, starting transfers between devices, shifted(): lax.ppermute(values, axis, [(i, i + step) for i in range(count) if 0 <= i...  7.51 us
  transfers between devices with their start and end apart: 9, of which 5 were waited for; matrix products, arithmetic and copies ran while one was open for 3% of the time, Pallas kernels for 17%

commit v1 on v0

--- a/solution.py
+++ b/solution.py
@@ -26,10 +26,15 @@
 BF16 = jnp.bfloat16
 VMEM = pl.BlockSpec(memory_space=pltpu.VMEM)
 SMEM = pl.BlockSpec(memory_space=pltpu.SMEM)
+ANY = pl.BlockSpec(memory_space=pl.ANY)
+DMA = pltpu.SemaphoreType.DMA
+SENT = 144
+SHARE = 72
+BACK = 168
 PARAMS = pltpu.CompilerParams(vmem_limit_bytes=56 * 1024 * 1024)
 
 
-def call(kernel, ins, out_shape, out_specs, scratch, flops, moved):
+def call(kernel, ins, out_shape, out_specs, scratch, flops, moved, **more):
     return pl.pallas_call(
         kernel,
         in_specs=ins,
@@ -38,6 +43,7 @@
         scratch_shapes=scratch,
         compiler_params=PARAMS,
         cost_estimate=pl.CostEstimate(flops=flops, bytes_accessed=moved, transcendentals=0),
+        **more,
     )
 
 
@@ -59,32 +65,66 @@
     first_ref,
     count_ref,
     live_ref,
-    route_ref,
+    dest_ref,
     feat_ref,
     weight_ref,
     slot_ref,
+    cell_ref,
     out_ref,
     table_ref,
+    route_ref,
     prob,
     part,
+    seen,
+    spread_cells,
+    code,
 ):
+    def clear(i, c):
+        seen[i] = 0
+        return c
+
+    lax.fori_loop(0, 128, clear, 0, unroll=8)
+
     def wipe(i, c):
-        out_ref[pl.ds(pl.multiple_of(i * 256, 256), 256), :] = jnp.zeros((256, CH), BF16)
+        out_ref[i] = jnp.zeros((SENT, 128), BF16)
         return c
 
-    lax.fori_loop(0, 32, wipe, 0)
+    lax.fori_loop(0, 128, wipe, 0)
+    code[...] = jnp.full_like(code, -1)
+    quarter = lax.broadcasted_iota(jnp.int32, (8, 128), 1) >> 5
+    for k in range(LISTS):
+        cells = cell_ref[:, k // 4 * 128 : k // 4 * 128 + 128]
+        one = jnp.where(quarter == k % 4, jnp.concatenate([cells, cells], axis=0), 0)
+        two = one + pltpu.roll(one, 32, 1)
+        spread_cells[k] = two + pltpu.roll(two, 64, 1)
+    half = (lax.broadcasted_iota(jnp.int32, (1, 128), 1) >> 5) & 1
+    for i in range(BLOCKS * LISTS):
+        b, k = i // LISTS, i % LISTS
+        tile = dest_ref[b, k]
+        rank = seen[tile]
+        seen[tile] = rank + 1
+        route_ref[i] = tile * CAP + rank
+        code[pl.ds(tile, 1), :] = jnp.where(
+            half == rank, spread_cells[k, b : b + 1, :], code[pl.ds(tile, 1), :]
+        )
+    row = lax.broadcasted_iota(jnp.int32, (16, 128), 0)
+    high, low = (code[...] >> 7).astype(F32), (code[...] & 127).astype(F32)
+    for d in range(128):
+        out_ref[d, 128:SENT, :] = jnp.where(
+            row == 0, high[d : d + 1, :], jnp.where(row == 1, low[d : d + 1, :], 0.0)
+        ).astype(BF16)
     low = lax.broadcasted_iota(jnp.int32, (8, LIVE), 0)
 
     def block(b, c):
         _, share, _ = depth_parts(first_ref, count_ref, weight_ref, b)
         prob[...] = share
         first = first_ref[b]
-        pairs = (count_ref[b] + 1) // 2
+        quads = (count_ref[b] + 3) // 4
         for chunk in range(4):
 
-            def pair(i, acc):
-                for step in range(2):
-                    d = first + 2 * i + step
+            def quad(i, acc):
+                for step in range(4):
+                    d = jnp.minimum(first + 4 * i + step, BINS - 1)
                     slot = jnp.broadcast_to(slot_ref[b, pl.ds(d, 1), :], (8, LIVE))
                     share = jnp.broadcast_to(prob[pl.ds(d, 1), :], (8, LIVE))
                     mine = jnp.where((slot & 7) == low, share, 0.0)
@@ -92,7 +132,7 @@
                     acc = [a + jnp.where(high == r, mine, 0.0) for r, a in enumerate(acc)]
                 return acc
 
-            acc = lax.fori_loop(0, pairs, pair, [jnp.zeros((8, LIVE), F32)] * 32)
+            acc = lax.fori_loop(0, quads, quad, [jnp.zeros((8, LIVE), F32)] * 32)
             table_ref[b, chunk * 256 : (chunk + 1) * 256, :] = jnp.concatenate(acc, axis=0).astype(
                 BF16
             )
@@ -100,80 +140,84 @@
             table_ref[b], masked_features(live_ref, feat_ref, b), preferred_element_type=F32
         ).astype(BF16)
         for k in range(LISTS):
-            to = pl.multiple_of(route_ref[b * LISTS + k] * LIST, LIST)
-            out_ref[pl.ds(to, LIST), :] = part[k * LIST : (k + 1) * LIST, :]
+            to = route_ref[b * LISTS + k]
+            for h in range(2):
+                at = pl.multiple_of((to & 1) * 64 + h * LIST, LIST)
+                out_ref[to >> 1, pl.ds(at, LIST), :] = part[
+                    k * LIST : (k + 1) * LIST, h * 128 : (h + 1) * 128
+                ]
         return c
 
     lax.fori_loop(0, BLOCKS, block, 0)
 
 
-def lift(first, count, live, route, features, weights, slots):
+def lift(first, count, live, dest, features, weights, slots, cells):
     return call(
         lift_kernel,
-        [SMEM] * 4 + [VMEM] * 3,
+        [SMEM] * 4 + [VMEM] * 4,
         (
-            jax.ShapeDtypeStruct((128 * CAP * LIST, CH), BF16),
+            jax.ShapeDtypeStruct((128, SENT, 128), BF16),
             jax.ShapeDtypeStruct((BLOCKS, SLOTS, LIVE), BF16),
+            jax.ShapeDtypeStruct((BLOCKS * LISTS,), jnp.int32),
         ),
-        (VMEM, VMEM),
-        [pltpu.VMEM((BINS, LIVE), F32), pltpu.VMEM((SLOTS, CH), BF16)],
+        (VMEM, VMEM, SMEM),
+        [
+            pltpu.VMEM((BINS, LIVE), F32),
+            pltpu.VMEM((SLOTS, CH), BF16),
+            pltpu.SMEM((128,), jnp.int32),
+            pltpu.VMEM((LISTS, 8, 128), jnp.int32),
+            pltpu.VMEM((128, 128), jnp.int32),
+        ],
         300_000_000,
         6_000_000,
-    )(first, count, live, route, features, weights, slots)
-
-
-def pack_kernel(dest_ref, cell_ref, out_ref, route_ref, seen):
-    def clear(i, c):
-        seen[i] = 0
-        return c
-
-    lax.fori_loop(0, 128, clear, 0, unroll=8)
-    out_ref[...] = jnp.full_like(out_ref, -1)
-    for i in range(BLOCKS * LISTS):
-        b, k = i // LISTS, i % LISTS
-        tile = dest_ref[b, k]
-        rank = seen[tile]
-        seen[tile] = rank + 1
-        to = tile * CAP + rank
-        route_ref[i] = to
-        out_ref[pl.ds(to, 1), :] = cell_ref[b : b + 1, k * LIST : (k + 1) * LIST]
-
-
-def packed_cells(dest, cells):
-    return call(
-        pack_kernel,
-        [SMEM, VMEM],
-        (
-            jax.ShapeDtypeStruct((128 * CAP, LIST), jnp.int32),
-            jax.ShapeDtypeStruct((BLOCKS * LISTS,), jnp.int32),
-        ),
-        (VMEM, SMEM),
-        [pltpu.SMEM((128,), jnp.int32)],
-        1_000_000,
-        100_000,
-    )(dest, cells)
+    )(first, count, live, dest, features, weights, slots, cells)
 
 
 def splat_kernel(
-    cell_ref, list_ref, gout_ref, base_ref, top_ref, bottom_ref, left_ref, right_ref, acc, hit, strip
+    list_ref,
+    gout_ref,
+    base_ref,
+    top_ref,
+    bottom_ref,
+    left_ref,
+    right_ref,
+    acc,
+    hit,
+    strip,
+    lists,
+    code,
 ):
     rows = 128
     span = 1024
     places = lax.broadcasted_iota(jnp.int32, (rows, span), 0).astype(F32).astype(BF16)
+    first_half = lax.broadcasted_iota(jnp.int32, (1, 128), 1) < 64
     one, zero = jnp.ones((), BF16), jnp.zeros((), BF16)
+    for n in range(64):
+        codes = [list_ref[2 * n + e, 128:SENT, :].astype(F32) for e in range(2)]
+        for i in range(2):
+            code[n // 8 * 2 + i : n // 8 * 2 + i + 1, n % 8 * 128 : n % 8 * 128 + 128] = jnp.where(
+                first_half, codes[0][i : i + 1, :], codes[1][i : i + 1, :]
+            )
     for chunk in range(8):
-        cells = cell_ref[chunk : chunk + 1, :]
-        low = jnp.broadcast_to((cells & 127).astype(F32), (rows, span)).astype(BF16)
-        high = jnp.broadcast_to((cells >> 7).astype(F32), (rows, span)).astype(BF16)
+        for n in range(16):
+            d = chunk * 16 + n
+            for r in range(CAP):
+                for h in range(2):
+                    at = (n * CAP + r) * LIST
+                    lists[at : at + LIST, h * 128 : (h + 1) * 128] = list_ref[
+                        d, r * 64 + h * LIST : r * 64 + (h + 1) * LIST, :
+                    ]
+        high, low = [
+            jnp.broadcast_to(code[2 * chunk + i : 2 * chunk + i + 1, :], (rows, span)).astype(BF16)
+            for i in range(2)
+        ]
         same = jnp.where(low == places, one, zero)
         for m in range(13):
             end = min(rows, CELLS - m * rows)
             hit[m * rows : m * rows + end, :] = jnp.where(
                 high == jnp.full((), m, BF16), same, zero
             )[:end, :]
-        part = jnp.dot(
-            hit[...], list_ref[chunk * span : (chunk + 1) * span, :], preferred_element_type=F32
-        )
+        part = jnp.dot(hit[...], lists[...], preferred_element_type=F32)
         if chunk == 0:
             acc[...] = part
         else:
@@ -190,17 +234,23 @@
         ref[80:, :] = gout_ref[n]
 
 
-def splat(cells, lists, gout_edges):
+def splat(lists, gout_edges):
     strip = jax.ShapeDtypeStruct((160, CH), BF16)
     return call(
         splat_kernel,
-        [VMEM] * 3,
+        [VMEM] * 2,
         (jax.ShapeDtypeStruct((CELLS, CH), BF16),) + (strip,) * 4,
         (VMEM,) * 5,
-        [pltpu.VMEM((CELLS, CH), F32), pltpu.VMEM((CELLS, 1024), BF16), pltpu.VMEM((2, 80, CH), F32)],
+        [
+            pltpu.VMEM((CELLS, CH), F32),
+            pltpu.VMEM((CELLS, 1024), BF16),
+            pltpu.VMEM((2, 80, CH), F32),
+            pltpu.VMEM((1024, CH), BF16),
+            pltpu.VMEM((16, 1024), F32),
+        ],
         6_700_000_000,
         6_000_000,
-    )(cells, lists, gout_edges)
+    )(lists, gout_edges)
 
 
 def corner_kernel(top_ref, bottom_ref, left_ref, right_ref, up_ref, down_ref):
@@ -308,18 +358,17 @@
             out[to : to + CH, :] = got[:, h * 128 : (h + 1) * 128]
 
 
-def turn(spot_ref, wide, turned):
+def turn(spot_ref, rows_at, turned):
     for k in range(WIDE // 256):
         at = WIDE0 + k * 256
         inside = place_mask(spot_ref[0], spot_ref[1], at, 256, 0)
-        values = wide[at : at + 256, CH : 2 * CH].astype(F32)
-        turned[:, k * 256 : (k + 1) * 256] = jnp.where(inside, values, 0.0).T.astype(BF16)
+        turned[:, k * 256 : (k + 1) * 256] = jnp.where(inside, rows_at(at), 0.0).T.astype(BF16)
 
 
 def act_kernel(
     spot_ref,
-    first_ref,
-    second_ref,
+    first_hbm,
+    second_hbm,
     base_ref,
     gout_ref,
     above_ref,
@@ -329,12 +378,21 @@
     hidden_ref,
     fcot_ref,
     sums_ref,
+    first_ref,
+    second_ref,
     wide,
     gwide,
     flat,
     flat2,
     turned,
+    arrive,
 ):
+    loads = (
+        pltpu.make_async_copy(first_hbm, first_ref, arrive.at[0]),
+        pltpu.make_async_copy(second_hbm, second_ref, arrive.at[1]),
+    )
+    for load in loads:
+        load.start()
     rims = (above_ref, below_ref, left_ref, right_ref)
     lay_out(flat, base_ref, *rims, 0)
     spread(flat, wide)
@@ -342,6 +400,8 @@
     spread(flat2, gwide)
     flat[...] = jnp.zeros_like(flat)
     flat2[...] = jnp.zeros_like(flat2)
+    for load in loads:
+        load.wait()
 
     def activate(k, c):
         at = pl.multiple_of(WIDE0 + k * 512, 16)
@@ -356,31 +416,41 @@
         return c
 
     lax.fori_loop(0, WIDE // 512, activate, 0)
-    spread(flat, fcot_ref)
-    turn(spot_ref, fcot_ref, turned)
+    fcot_ref[...] = flat[8 : 8 + FLAT, :].astype(BF16)
+    hidden_ref[...] = flat2[8 : 8 + FLAT, :].astype(BF16)
+    turn(spot_ref, lambda at: flat[at + 8 : at + 264, :], turned)
     kernel_sums(wide, turned, sums_ref.at[0])
-    spread(flat2, hidden_ref)
-    turn(spot_ref, gwide, turned)
-    kernel_sums(hidden_ref, turned, sums_ref.at[1])
+    spread(flat2, wide)
+    turn(spot_ref, lambda at: gwide[at : at + 256, CH : 2 * CH].astype(F32), turned)
+    kernel_sums(wide, turned, sums_ref.at[1])
 
 
 def activate_tile(spot, first, second, base, gout, rims):
-    wide = jax.ShapeDtypeStruct((FLAT, 3 * CH), BF16)
+    flat = jax.ShapeDtypeStruct((FLAT, CH), BF16)
     return call(
         act_kernel,
-        [SMEM] + [VMEM] * 8,
-        (wide, wide, jax.ShapeDtypeStruct((2, 18 * CH, 128), BF16)),
+        [SMEM, ANY, ANY] + [VMEM] * 6,
+        (flat, flat, jax.ShapeDtypeStruct((2, 18 * CH, 128), BF16)),
         (VMEM,) * 3,
         [
+            pltpu.VMEM((9 * CH, CH), BF16),
+            pltpu.VMEM((9 * CH, CH), BF16),
             pltpu.VMEM((FLAT, 3 * CH), BF16),
             pltpu.VMEM((FLAT, 3 * CH), BF16),
             pltpu.VMEM((FLAT + 16, CH), F32),
             pltpu.VMEM((FLAT + 16, CH), F32),
             pltpu.VMEM((CH, WIDE), BF16),
+            DMA((2,)),
         ],
         9_000_000_000,
-        16_000_000,
+        9_000_000,
     )(spot, first, second, base, gout, *rims)
+
+
+def respread(values_ref, flat, wide):
+    flat[...] = jnp.zeros_like(flat)
+    flat[8 : 8 + FLAT, :] = values_ref[...].astype(F32)
+    spread(flat, wide)
 
 
 def strip_pads(got, out, k):
@@ -390,10 +460,12 @@
         out[pl.ds(to, 80), :] = jnp.concatenate(lines, axis=0).astype(BF16)
 
 
-def back_kernel(first_ref, cell_ref, fcot_ref, out_ref, tile):
+def back_kernel(first_ref, cell_ref, fcot_ref, out_ref, tile, flat, wide):
+    respread(fcot_ref, flat, wide)
+
     def back(k, c):
         at = pl.multiple_of(CORE0 + k * 480, 16)
-        strip_pads(taps(fcot_ref, first_ref, at, 480), tile, k)
+        strip_pads(taps(wide, first_ref, at, 480), tile, k)
         return c
 
     lax.fori_loop(0, 4, back, 0)
@@ -407,30 +479,49 @@
         high = (cells >> 7).astype(F32).astype(BF16)
         same = jnp.where((cells & 127).astype(F32).astype(BF16) == places, one, zero)
         hits = [jnp.where(high == jnp.full((), m, BF16), same, zero) for m in range(13)]
-        out_ref[pl.ds(at, 512), :] = jnp.dot(
+        got = jnp.dot(
             jnp.concatenate(hits, axis=1), tile[...], preferred_element_type=F32
         ).astype(BF16)
+        for n in range(16):
+            for h in range(2):
+                at = (n % 2) * 64 + h * LIST
+                out_ref[k * 8 + n // 2, at : at + LIST, :] = got[
+                    n * LIST : (n + 1) * LIST, h * 128 : (h + 1) * 128
+                ]
         return c
 
     lax.fori_loop(0, 16, pick, 0)
 
 
-def send_back(first, cells, fcot_wide):
+def send_back(first, cells, fcot):
     return call(
         back_kernel,
         [VMEM] * 3,
-        jax.ShapeDtypeStruct((128 * CAP * LIST, CH), BF16),
+        jax.ShapeDtypeStruct((128, BACK, 128), BF16),
         VMEM,
-        [pltpu.VMEM((1664, CH), BF16)],
+        [
+            pltpu.VMEM((1664, CH), BF16),
+            pltpu.VMEM((FLAT + 16, CH), F32),
+            pltpu.VMEM((FLAT, 3 * CH), BF16),
+        ],
         9_000_000_000,
         12_000_000,
-    )(first, cells, fcot_wide)
-
-
-def out_kernel(second_ref, hidden_ref, out_ref):
+    )(first, cells, fcot)
+
+
+def add_share(parts, back):
+    total = jnp.sum(parts.astype(F32), axis=0)
+    halves = jnp.stack([total[:40], total[32:]]).astype(BF16)
+    beside = jnp.broadcast_to(halves, (64, 2, 40, 128)).reshape(128, 40, 128)
+    return lax.dynamic_update_slice(back, beside, (0, 128, 0))
+
+
+def out_kernel(second_ref, hidden_ref, out_ref, flat, wide):
+    respread(hidden_ref, flat, wide)
+
     def forward(k, c):
         at = pl.multiple_of(CORE0 + k * 480, 16)
-        strip_pads(taps(hidden_ref, second_ref, at, 480), out_ref, k)
+        strip_pads(taps(wide, second_ref, at, 480), out_ref, k)
         return c
 
     lax.fori_loop(0, 4, forward, 0)
@@ -442,43 +533,81 @@
         [VMEM] * 2,
         jax.ShapeDtypeStruct((CELLS, CH), BF16),
         VMEM,
-        [],
+        [pltpu.VMEM((FLAT + 16, CH), F32), pltpu.VMEM((FLAT, 3 * CH), BF16)],
         2_300_000_000,
         5_000_000,
     )(second, hidden_wide)
 
 
-def widen_kernel(sums_ref, one_ref, two_ref):
-    for by in range(16):
-        for bx in range(8):
-            values = sums_ref[bx, by].astype(F32)
-            at = (by * 8 + bx) * 72
-            done = 0
-            while done < 72:
-                part, row = divmod(at + done, CH)
-                n, part = divmod(part, 18)
-                size = min(72 - done, CH - row)
-                out = (one_ref, two_ref)[n]
-                lanes = slice(part % 2 * 128, part % 2 * 128 + 128)
-                out[part // 2, row : row + size, lanes] = values[done : done + size, :]
-                done += size
-
-
-def widen(sums):
+def widen_kernel(spot_ref, own_ref, other_ref, one_hbm, two_hbm, one, two, sent):
+    odd = spot_ref[1] % 2 == 1
+    copies = [
+        pltpu.make_async_copy(wide.at[tap], hbm.at[tap], sent.at[9 * n + tap])
+        for n, (wide, hbm) in enumerate(((one, one_hbm), (two, two_hbm)))
+        for tap in range(9)
+    ]
+    for device in range(128):
+        own, other = own_ref[device].astype(F32), other_ref[device].astype(F32)
+        low, high = jnp.where(odd, other, own), jnp.where(odd, own, other)
+        values = jnp.concatenate([low, high[8:, :]], axis=0)
+        done = 0
+        while done < SHARE:
+            part, row = divmod(device * SHARE + done, CH)
+            n, part = divmod(part, 18)
+            size = min(SHARE - done, CH - row)
+            lanes = slice(part % 2 * 128, part % 2 * 128 + 128)
+            (one, two)[n][part // 2, row : row + size, lanes] = values[done : done + size, :]
+            done += size
+            if row + size == CH and part % 2 == 1:
+                copies[9 * n + part // 2].start()
+    for copy in copies:
+        copy.wait()
+
+
+def widen(spot, own, other):
     out = jax.ShapeDtypeStruct((9, CH, CH), F32)
-    return call(widen_kernel, [VMEM], (out, out), (VMEM, VMEM), [], 1_000_000, 7_000_000)(sums)
-
-
-def settle_kernel(first_ref, count_ref, live_ref, route_ref, feat_ref, weight_ref, slot_ref, table_ref, back_ref, gfeat_ref, gweight_ref, part, cot, pick):
+    wide = pltpu.VMEM((9, CH, CH), F32)
+    return call(
+        widen_kernel,
+        [SMEM, VMEM, VMEM],
+        (out, out),
+        (ANY, ANY),
+        [wide, wide, DMA((18,))],
+        1_000_000,
+        7_000_000,
+    )(spot, own, other)
+
+
+def settle_kernel(
+    first_ref,
+    count_ref,
+    live_ref,
+    route_ref,
+    feat_ref,
+    weight_ref,
+    slot_ref,
+    table_ref,
+    back_ref,
+    gfeat_ref,
+    gweight_ref,
+    part,
+    cot,
+    pick,
+):
     for b in range(BLOCKS):
         for k in range(LISTS):
-            at = pl.multiple_of(route_ref[b * LISTS + k] * LIST, LIST)
-            part[k * LIST : (k + 1) * LIST, :] = back_ref[pl.ds(at, LIST), :]
+            to = route_ref[b * LISTS + k]
+            rows = pl.ds(pl.multiple_of((to & 1) * 64, 64), 64)
+            part[b * LISTS + k] = back_ref[to >> 1, rows, :]
+        got = part[b * LISTS : (b + 1) * LISTS]
+        lists = jnp.concatenate(
+            [got[:, h * LIST : (h + 1) * LIST, :].reshape(SLOTS, 128) for h in range(2)], axis=1
+        )
         masked = masked_features(live_ref, feat_ref, b)
         cot[...] = lax.dot_general(
-            part[...], masked, (((1,), (1,)), ((), ())), preferred_element_type=F32
+            lists, masked, (((1,), (1,)), ((), ())), preferred_element_type=F32
         )
-        got = jnp.dot(table_ref[b], part[...], preferred_element_type=F32)
+        got = jnp.dot(table_ref[b], lists, preferred_element_type=F32)
         patch = lax.broadcasted_iota(jnp.int32, (LIVE, CH), 0)
         gfeat_ref[b] = jnp.where(patch < live_ref[b], got, 0.0).astype(BF16)
         pick[...] = jnp.zeros_like(pick)
@@ -517,7 +646,7 @@
         ),
         (VMEM, VMEM),
         [
-            pltpu.VMEM((SLOTS, CH), BF16),
+            pltpu.VMEM((BLOCKS * LISTS, CAP * LIST, 128), BF16),
             pltpu.VMEM((SLOTS, LIVE), F32),
             pltpu.VMEM((BINS, LIVE), F32),
         ],
@@ -547,15 +676,18 @@
     me = by * lax.axis_size("bx") + bx
     devices = lax.axis_size("by") * lax.axis_size("bx")
     spot = jnp.stack([by, bx]).astype(jnp.int32)
-    groups = BLOCKS * LISTS
     first_taps = conv_first.reshape(9 * CH, CH)
     second_taps = conv_second.reshape(9 * CH, CH)
 
-    cells, route = packed_cells(tile_dest, tile_cells)
-    cells = exchanged(cells.reshape(devices, CAP, LIST)).reshape(devices * CAP * LIST)
-    cell_column = cells.reshape(-1, 1)
-    outgoing, table = lift(
-        depth_first, depth_count, patch_count, route, features, depth_weight, depth_slot
+    outgoing, table, route = lift(
+        depth_first,
+        depth_count,
+        patch_count,
+        tile_dest,
+        features,
+        depth_weight,
+        depth_slot,
+        tile_cells,
     )
     arrived = exchanged(outgoing)
 
@@ -571,29 +703,28 @@
     turned_table = jnp.swapaxes(table, 1, 2)
     _, first_late, second_late = lax.optimization_barrier((outgoing, first_taps, second_taps))
     first_flip, second_flip = flipped(first_late, second_late)
-    arrived, cell_column, turned_table, first_flip, second_flip = lax.optimization_barrier(
-        (arrived, cell_column, turned_table, first_flip, second_flip)
-    )
-
-    base, top, bottom, left, right = splat(cells.reshape(8, 1024), arrived, gout_edges)
+    arrived, turned_table, first_flip, second_flip = lax.optimization_barrier(
+        (arrived, turned_table, first_flip, second_flip)
+    )
+
+    base, top, bottom, left, right = splat(arrived, gout_edges)
     from_left, from_right = shifted(right, "bx", 1), shifted(left, "bx", -1)
     up, down = with_corners(top, bottom, from_left, from_right)
     rims = (shifted(down, "by", 1), shifted(up, "by", -1), from_left, from_right)
-    hidden_wide, fcot_wide, sums = activate_tile(
+    hidden, fcot, sums = activate_tile(
         spot, first_taps, second_flip, base, grad_out.reshape(CELLS, CH), rims
     )
-    sums = exchanged(sums.reshape(devices, 72, 128))
-    returning = send_back(first_flip, cell_column, fcot_wide)
-    returning, sums = lax.optimization_barrier((returning, sums))
-    sums = jnp.sum(sums.astype(F32), axis=0).astype(BF16)
-    sums = lax.all_to_all(
-        jnp.broadcast_to(sums, (16, 72, 128)), "by", split_axis=0, concat_axis=0, tiled=True
-    )
-    returning, sums = lax.optimization_barrier((returning, sums))
-    sums = lax.all_gather(sums, "bx", axis=0)
-    returned = exchanged(returning)
-    out_bev = outward(second_taps, hidden_wide)
+    arrived, sums = lax.optimization_barrier((arrived, sums))
+    codes = arrived[:, 128:130, :64].astype(F32)
+    cell_column = (codes[:, 0] * 128 + codes[:, 1]).astype(jnp.int32).reshape(-1, 1)
+    pairs = [(i, i ^ 1) for i in range(lax.axis_size("bx"))]
+    sums = exchanged(sums.reshape(devices, SHARE, 128))
+    returning = send_back(first_flip, cell_column, fcot)
+    returned = exchanged(add_share(sums, returning))
+    out_bev = outward(second_taps, hidden)
     returned, out_bev = lax.optimization_barrier((returned, out_bev))
+    own = returned[:, 128:, :]
+    other = lax.ppermute(own, "bx", pairs)
     feature_grad, weight_grad = settle(
         depth_first,
         depth_count,
@@ -605,8 +736,8 @@
         turned_table,
         returned,
     )
-    sums, weight_grad = lax.optimization_barrier((sums, weight_grad))
-    grad_first, grad_second = widen(sums)
+    other, weight_grad = lax.optimization_barrier((other, weight_grad))
+    grad_first, grad_second = widen(spot, own, other)
     return (
         out_bev.reshape(TILE, TILE, CH),
         feature_grad,

time: 286 us -> 268 us (0.937)
  between operations: 14.2 us -> 1 us
  blocking collectives: 11.4 us -> 0 us
  waiting for transfers between devices: 116 us -> 126 us
  starting transfers between devices: 47 us -> 37.3 us
  local copies, waits for them, and re-layouts: 8.21 us -> 14.2 us
    all_to_all x1 -> x0, blocking collectives: 11.4 us -> none  [on_device(): lax.all_to_all(jnp.broadcast_to(sums, (16, 72, 128)), 'by', split_axis=0,...]
    all_to_all x4 -> x3, waiting for transfers between devices: 107 us -> 118 us  [exchanged(): lax.all_to_all(values, ('by', 'bx'), split_axis=0, concat_axis=0, tiled=T...]
    all_to_all x4 -> x3, starting transfers between devices: 39.5 us -> 28.9 us  [exchanged(): lax.all_to_all(values, ('by', 'bx'), split_axis=0, concat_axis=0, tiled=T...]
    convert_element_type x0 -> x1, local copies, waits for them, and re-layouts: none -> 5.66 us  [on_device(): (codes[:, 0] * 128 + codes[:, 1]).astype(jnp.int32).reshape(-1, 1)]
    pallas_call x6 -> x5, Pallas kernels: 68.6 us -> 67.5 us  [the longest x1 20.2 us: send_back(): call(back_kernel, [VMEM] * 3, jax.ShapeDtypeStruct((128, BACK, 128), BF16...]
  transfers between devices with their start and end apart: 9 -> 8, of which waited for: 5 -> 5; matrix products, arithmetic and copies ran while one was open for 3% -> 4% of each run, Pallas kernels for 17% -> 14%
where the time goes in v1:
time: 268 us; the launch traced here: 267 us
  waiting for transfers between devices  126 us (47%)
  Pallas kernels  86.2 us (32%)
  starting transfers between devices  37.3 us (14%)
  local copies, waits for them, and re-layouts  14.2 us (5%)
  other arithmetic  2.95 us (1%)
    all_to_all x3, waiting for transfers between devices, exchanged(): lax.all_to_all(values, ('by', 'bx'), split_axis=0, concat_axis=0, tiled=T...  118 us
    all_to_all x3, starting transfers between devices, exchanged(): lax.all_to_all(values, ('by', 'bx'), split_axis=0, concat_axis=0, tiled=T...  28.9 us
    pallas_call x1, Pallas kernels, send_back(): call(back_kernel, [VMEM] * 3, jax.ShapeDtypeStruct((128, BACK, 128), BF16...  20.2 us
    pallas_call x1, Pallas kernels, activate_tile(): call(act_kernel, [SMEM, ANY, ANY] + [VMEM] * 6, (flat, flat, jax.ShapeDty...  18.5 us
    pallas_call x1, Pallas kernels, lift(): call(lift_kernel, [SMEM] * 4 + [VMEM] * 4, (jax.ShapeDtypeStruct((128, SE...  13.5 us
    pallas_call x1, Pallas kernels, splat(): call(splat_kernel, [VMEM] * 2, (jax.ShapeDtypeStruct((CELLS, CH), BF16),)...  11.2 us
    ppermute x4, starting transfers between devices, shifted(): lax.ppermute(values, axis, [(i, i + step) for i in range(count) if 0 <= i...  7.52 us
    ppermute x4, waiting for transfers between devices, shifted(): lax.ppermute(values, axis, [(i, i + step) for i in range(count) if 0 <= i...  7.5 us
  transfers between devices with their start and end apart: 8, of which 5 were waited for; matrix products, arithmetic and copies ran while one was open for 4% of the time, Pallas kernels for 14%

profile of v1, /device:TPU:1, one launch (start us, length us, event | category | flops | bytes accessed | tf_op | source)
XLA Modules:
  0.0 267.3 jit_solution(8122046532753040391)
XLA Ops:
  0.6 13.5 %shard_map.146 = (bf16[128,144,128]{2,1,0:T(8,128)(2,1)}, bf16[4,1024,128]{2,1,0:T(8,128)(2,1)}, s32[128]{0:T(128)}) custom-call(s32[4]{0:T(128)} %first_ref.3, s32[4]{0:T(128)} %count_ref.3, s32[4]{0:T(128)} %live_ref.3, s32[4,32]{1,0:T(4,128)} %dest_ref.1, bf16[4,128,256]{2,1,0:T(8,128)(2,1)} %feat_ref.3, f32[4,64,128]{2,1,0:T(8,128)} %weight_ref.3, ...), custom_call_target="tpu_custom_call" | custom-call | flops 300000000 | bytes 6000000 | tf_op jit(solution)/shard_map/pallas_call | solution.py:155
  14.2 13.5 %all-to-all-start = ((bf16[128,144,128]{2,1,0:T(8,128)(2,1)}), bf16[128,144,128]{2,1,0:T(8,128)(2,1)}, u32[]{:S(2)}, u32[]{:S(2)}) async-start(bf16[128,144,128]{2,1,0:T(8,128)(2,1)} %get-tuple-element.37), calls=%async_computation | async-start | bytes 9437184 | tf_op jit(solution)/shard_map/all_to_all | solution.py:659
  27.7 1.3 copy.17
  30.1 3.4 %shard_map.147 = (bf16[2304,256]{1,0:T(8,128)(2,1)}, bf16[2304,256]{1,0:T(8,128)(2,1)}) custom-call(bf16[2304,256]{1,0:T(8,128)(2,1)} %bitcast.20, bf16[2304,256]{1,0:T(8,128)(2,1)} %bitcast.22), custom_call_target="tpu_custom_call" | custom-call | flops 10000000 | bytes 5000000 | tf_op jit(solution)/shard_map/pallas_call | solution.py:333
  35.1 51.1 %all-to-all-done.list_ref = bf16[128,144,128]{2,1,0:T(8,128)(2,1)} async-done(((bf16[128,144,128]{2,1,0:T(8,128)(2,1)}), bf16[128,144,128]{2,1,0:T(8,128)(2,1)}, u32[]{:S(2)}, u32[]{:S(2)}) %all-to-all-start) | async-done | bytes 4718624 | tf_op jit(solution)/shard_map/all_to_all | solution.py:659
  86.2 11.2 %shard_map.148 = (bf16[1600,256]{1,0:T(8,128)(2,1)}, bf16[160,256]{1,0:T(8,128)(2,1)}, bf16[160,256]{1,0:T(8,128)(2,1)}, bf16[160,256]{1,0:T(8,128)(2,1)}, bf16[160,256]{1,0:T(8,128)(2,1)}) custom-call(bf16[128,144,128]{2,1,0:T(8,128)(2,1)} %all-to-all-done.list_ref, bf16[4,80,256]{2,1,0:T(8,128)(2,1)} %pad_maximum_fusion.gout_ref), custom_call_target="tpu_custom_call" | custom-call | flops 6700000256 | bytes 6000000 | tf_op jit(solution)/shard_map/pallas_call | solution.py:239
  97.3 2.8 %collective-permute-start = (bf16[160,256]{1,0:T(8,128)(2,1)}, bf16[160,256]{1,0:T(8,128)(2,1)S(1)}, u32[]{:S(2)}, u32[]{:S(2)}) collective-permute-start(bf16[160,256]{1,0:T(8,128)(2,1)} %get-tuple-element.50), channel_id=1, source_target_pairs={{0,1},{1,2},{2,3},{3,4},{4,5},{5,6},{6,7},{8,9},{9,10},{10,11},{11... | collective-permute-start | bytes 245768 | tf_op jit(solution)/shard_map/ppermute | solution.py:276
  100.2 1.9 collective-permute-start.1
  102.1 4.0 %collective-permute-done.1.right_ref = bf16[160,256]{1,0:T(8,128)(2,1)S(1)} collective-permute-done((bf16[160,256]{1,0:T(8,128)(2,1)}, bf16[160,256]{1,0:T(8,128)(2,1)S(1)}, u32[]{:S(2)}, u32[]{:S(2)}) %collective-permute-start.1) | collective-permute-done | bytes 81952 | tf_op jit(solution)/shard_map/ppermute | solution.py:276
  106.8 1.7 shard_map.149
  109.8 1.5 collective-permute-start.3
  111.9 3.5 %collective-permute-done.3.below_ref = bf16[192,256]{1,0:T(8,128)(2,1)S(1)} collective-permute-done((bf16[192,256]{1,0:T(8,128)(2,1)}, bf16[192,256]{1,0:T(8,128)(2,1)S(1)}, u32[]{:S(2)}, u32[]{:S(2)}) %collective-permute-start.3) | collective-permute-done | bytes 98336 | tf_op jit(solution)/shard_map/ppermute | solution.py:276
  116.0 18.5 %shard_map.150 = (bf16[2160,256]{1,0:T(8,128)(2,1)}, bf16[2160,256]{1,0:T(8,128)(2,1)}, bf16[2,4608,128]{2,1,0:T(8,128)(2,1)}) custom-call(s32[2]{0:T(128)} %pad_add_fusion.spot_ref, bf16[2304,256]{1,0:T(8,128)(2,1)} %bitcast.21, bf16[2304,256]{1,0:T(8,128)(2,1)} %get-tuple-element.45.second_hbm, bf16[1600,256]{1,0:T(8,128)(2,1)} %get-tuple-element.47.base_ref, ...), custom_call_target="tpu_custom_call" | custom-call | flops 8999999488 | bytes 9000000 | tf_op jit(solution)/shard_map/pallas_call | solution.py:430
  134.5 9.9 %all-to-all-start.1 = ((bf16[128,72,128]{2,1,0:T(8,128)(2,1)}), bf16[128,72,128]{2,1,0:T(8,128)(2,1)S(1)}, u32[]{:S(2)}, u32[]{:S(2)}) async-start(bf16[128,72,128]{2,1,0:T(8,128)(2,1)} %bitcast.19), calls=%async_computation.1 | async-start | bytes 4718592 | tf_op jit(solution)/shard_map/all_to_all | solution.py:659
  145.7 5.7 %convert_element_type.24.cell_ref = s32[8192,1]{1,0:T(8,128)} reshape(s32[128,64]{1,0:T(8,128)S(1)} %fusion.1) | data formatting | bytes 65536 | tf_op jit(solution)/shard_map/convert_element_type | solution.py:719
  151.3 20.2 %shard_map.151 = bf16[128,168,128]{2,1,0:T(8,128)(2,1)} custom-call(bf16[2304,256]{1,0:T(8,128)(2,1)} %get-tuple-element.43.first_ref, s32[8192,1]{1,0:T(8,128)} %convert_element_type.24.cell_ref, bf16[2160,256]{1,0:T(8,128)(2,1)} %get-tuple-element.56.fcot_ref), custom_call_target="tpu_custom_call" | custom-call | flops 8999999488 | bytes 12000000 | tf_op jit(solution)/shard_map/pallas_call | solution.py:497
  171.6 6.1 %all-to-all-done.1 = bf16[128,72,128]{2,1,0:T(8,128)(2,1)S(1)} async-done(((bf16[128,72,128]{2,1,0:T(8,128)(2,1)}), bf16[128,72,128]{2,1,0:T(8,128)(2,1)S(1)}, u32[]{:S(2)}, u32[]{:S(2)}) %all-to-all-start.1) | async-done | bytes 2359328 | tf_op jit(solution)/shard_map/all_to_all | solution.py:659
  178.3 1.4 constant_dynamic-update-slice_fusion
  179.7 5.5 %all-to-all-start.2 = ((bf16[128,168,128]{2,1,0:T(8,128)(2,1)}), bf16[128,168,128]{2,1,0:T(8,128)(2,1)}, u32[]{:S(2)}, u32[]{:S(2)}) async-start(bf16[128,168,128]{2,1,0:T(8,128)(2,1)} %constant_dynamic-update-slice_fusion), calls=%async_computation.2 | async-start | bytes 11010048 | tf_op jit(solution)/shard_map/all_to_all | solution.py:659
  185.2 6.1 %shard_map.152 = bf16[1600,256]{1,0:T(8,128)(2,1)} custom-call(bf16[2304,256]{1,0:T(8,128)(2,1)} %bitcast.23, bf16[2160,256]{1,0:T(8,128)(2,1)} %get-tuple-element.58.hidden_ref), custom_call_target="tpu_custom_call" | custom-call | flops 2300000000 | bytes 5000000 | tf_op jit(solution)/shard_map/pallas_call | solution.py:531
  191.3 60.9 %all-to-all-done.2.back_ref = bf16[128,168,128]{2,1,0:T(8,128)(2,1)} async-done(((bf16[128,168,128]{2,1,0:T(8,128)(2,1)}), bf16[128,168,128]{2,1,0:T(8,128)(2,1)}, u32[]{:S(2)}, u32[]{:S(2)}) %all-to-all-start.2) | async-done | bytes 5505056 | tf_op jit(solution)/shard_map/all_to_all | solution.py:659
  252.2 1.4 slice.41.own_ref
  254.6 7.4 %shard_map.153 = (bf16[4,128,256]{2,1,0:T(8,128)(2,1)}, f32[4,64,128]{2,1,0:T(8,128)}) custom-call(s32[4]{0:T(128)} %first_ref.3, s32[4]{0:T(128)} %count_ref.3, s32[4]{0:T(128)} %live_ref.3, s32[128]{0:T(128)} %get-tuple-element.60.route_ref, bf16[4,128,256]{2,1,0:T(8,128)(2,1)} %feat_ref.3, f32[4,64,128]{2,1,0:T(8,128)} %weight_ref.3, ...), custom_call_target="tpu_custom_call" | custom-call | flops 600000000 | bytes 8000000 | tf_op jit(solution)/shard_map/pallas_call | solution.py:640
  263.1 4.1 %shard_map.154 = (f32[9,256,256]{2,1,0:T(8,128)}, f32[9,256,256]{2,1,0:T(8,128)}) custom-call(s32[2]{0:T(128)} %pad_add_fusion.spot_ref, bf16[128,40,128]{2,1,0:T(8,128)(2,1)} %copy-done, bf16[128,40,128]{2,1,0:T(8,128)(2,1)} %copy-done.1), custom_call_target="tpu_custom_call" | custom-call | flops 1000000 | bytes 7000000 | tf_op jit(solution)/shard_map/pallas_call | solution.py:570
  (31 shorter events, 9.6 us)
Async XLA Ops:
  14.2 13.5 %copy-start.2 = (bf16[4,1024,128]{2,1,0:T(8,128)(2,1)S(1)}, bf16[4,1024,128]{2,1,0:T(8,128)(2,1)}, u32[]{:S(2)}) copy-start(bf16[4,1024,128]{2,1,0:T(8,128)(2,1)} %get-tuple-element.38) | copy-start | bytes 3145732
  14.2 72.0 %all-to-all-start = ((bf16[128,144,128]{2,1,0:T(8,128)(2,1)}), bf16[128,144,128]{2,1,0:T(8,128)(2,1)}, u32[]{:S(2)}, u32[]{:S(2)}) async-start(bf16[128,144,128]{2,1,0:T(8,128)(2,1)} %get-tuple-element.37), calls=%async_computation | async-start | bytes 9437184 | tf_op jit(solution)/shard_map/all_to_all | solution.py:659
  97.3 4.8 %collective-permute-start = (bf16[160,256]{1,0:T(8,128)(2,1)}, bf16[160,256]{1,0:T(8,128)(2,1)S(1)}, u32[]{:S(2)}, u32[]{:S(2)}) collective-permute-start(bf16[160,256]{1,0:T(8,128)(2,1)} %get-tuple-element.50), channel_id=1, source_target_pairs={{0,1},{1,2},{2,3},{3,4},{4,5},{5,6},{6,7},{8,9},{9,10},{10,11},{11... | collective-permute-start | bytes 245768 | tf_op jit(solution)/shard_map/ppermute | solution.py:276
  100.2 6.0 %collective-permute-start.1 = (bf16[160,256]{1,0:T(8,128)(2,1)}, bf16[160,256]{1,0:T(8,128)(2,1)S(1)}, u32[]{:S(2)}, u32[]{:S(2)}) collective-permute-start(bf16[160,256]{1,0:T(8,128)(2,1)} %get-tuple-element.51), channel_id=1, source_target_pairs={{1,0},{2,1},{3,2},{4,3},{5,4},{6,5},{7,6},{9,8},{10,9},{11,10},{12... | collective-permute-start | bytes 245768 | tf_op jit(solution)/shard_map/ppermute | solution.py:276
  102.1 4.0 %copy-start.3 = (bf16[160,256]{1,0:T(8,128)(2,1)}, bf16[160,256]{1,0:T(8,128)(2,1)S(1)}, u32[]{:S(2)}) copy-start(bf16[160,256]{1,0:T(8,128)(2,1)S(1)} %collective-permute-done.left_ref) | copy-start | bytes 245764
  106.2 0.6 copy-start.4
  108.5 3.4 %collective-permute-start.2 = (bf16[192,256]{1,0:T(8,128)(2,1)}, bf16[192,256]{1,0:T(8,128)(2,1)S(1)}, u32[]{:S(2)}, u32[]{:S(2)}) collective-permute-start(bf16[192,256]{1,0:T(8,128)(2,1)} %get-tuple-element.52), channel_id=1, source_target_pairs={{0,8},{8,16},{16,24},{24,32},{32,40},{40,48},{48,56},{56,64},{64,7... | collective-permute-start | bytes 294920 | tf_op jit(solution)/shard_map/ppermute | solution.py:276
  109.8 5.6 %collective-permute-start.3 = (bf16[192,256]{1,0:T(8,128)(2,1)}, bf16[192,256]{1,0:T(8,128)(2,1)S(1)}, u32[]{:S(2)}, u32[]{:S(2)}) collective-permute-start(bf16[192,256]{1,0:T(8,128)(2,1)} %get-tuple-element.53), channel_id=1, source_target_pairs={{8,0},{16,8},{24,16},{32,24},{40,32},{48,40},{56,48},{64,56},{72,6... | collective-permute-start | bytes 294920 | tf_op jit(solution)/shard_map/ppermute | solution.py:276
  111.9 3.5 %copy-start.5 = (bf16[192,256]{1,0:T(8,128)(2,1)}, bf16[192,256]{1,0:T(8,128)(2,1)S(1)}, u32[]{:S(2)}) copy-start(bf16[192,256]{1,0:T(8,128)(2,1)S(1)} %collective-permute-done.2.above_ref) | copy-start | bytes 294916
  115.3 0.6 copy-start.6
  134.5 43.2 %all-to-all-start.1 = ((bf16[128,72,128]{2,1,0:T(8,128)(2,1)}), bf16[128,72,128]{2,1,0:T(8,128)(2,1)S(1)}, u32[]{:S(2)}, u32[]{:S(2)}) async-start(bf16[128,72,128]{2,1,0:T(8,128)(2,1)} %bitcast.19), calls=%async_computation.1 | async-start | bytes 4718592 | tf_op jit(solution)/shard_map/all_to_all | solution.py:659
  179.7 72.6 %all-to-all-start.2 = ((bf16[128,168,128]{2,1,0:T(8,128)(2,1)}), bf16[128,168,128]{2,1,0:T(8,128)(2,1)}, u32[]{:S(2)}, u32[]{:S(2)}) async-start(bf16[128,168,128]{2,1,0:T(8,128)(2,1)} %constant_dynamic-update-slice_fusion), calls=%async_computation.2 | async-start | bytes 11010048 | tf_op jit(solution)/shard_map/all_to_all | solution.py:659
  253.7 8.3 %copy-start = (bf16[128,40,128]{2,1,0:T(8,128)(2,1)}, bf16[128,40,128]{2,1,0:T(8,128)(2,1)S(1)}, u32[]{:S(2)}) copy-start(bf16[128,40,128]{2,1,0:T(8,128)(2,1)S(1)} %slice.41.own_ref) | copy-start | bytes 3932164
  253.7 8.3 %collective-permute-start.4 = (bf16[128,40,128]{2,1,0:T(8,128)(2,1)S(1)}, bf16[128,40,128]{2,1,0:T(8,128)(2,1)S(1)}, u32[]{:S(2)}, u32[]{:S(2)}) collective-permute-start(bf16[128,40,128]{2,1,0:T(8,128)(2,1)S(1)} %slice.41.own_ref), channel_id=1, source_target_pairs={{0,1},{1,0},{2,3},{3,2},{4,5},{5,4},{6,7},{7,6},{8,9},{9,8},{10,11... | collective-permute-start | bytes 3932168 | tf_op jit(solution)/shard_map/ppermute | solution.py:727
  262.0 1.1 copy-start.1

commit v2 on v1

--- a/solution.py
+++ b/solution.py
@@ -28,7 +28,7 @@
 SMEM = pl.BlockSpec(memory_space=pltpu.SMEM)
 ANY = pl.BlockSpec(memory_space=pl.ANY)
 DMA = pltpu.SemaphoreType.DMA
-SENT = 144
+SENT = 136
 SHARE = 72
 BACK = 168
 PARAMS = pltpu.CompilerParams(vmem_limit_bytes=56 * 1024 * 1024)
@@ -85,11 +85,6 @@
 
     lax.fori_loop(0, 128, clear, 0, unroll=8)
 
-    def wipe(i, c):
-        out_ref[i] = jnp.zeros((SENT, 128), BF16)
-        return c
-
-    lax.fori_loop(0, 128, wipe, 0)
     code[...] = jnp.full_like(code, -1)
     quarter = lax.broadcasted_iota(jnp.int32, (8, 128), 1) >> 5
     for k in range(LISTS):
@@ -107,13 +102,13 @@
         code[pl.ds(tile, 1), :] = jnp.where(
             half == rank, spread_cells[k, b : b + 1, :], code[pl.ds(tile, 1), :]
         )
-    row = lax.broadcasted_iota(jnp.int32, (16, 128), 0)
+    row = lax.broadcasted_iota(jnp.int32, (8, 128), 0)
     high, low = (code[...] >> 7).astype(F32), (code[...] & 127).astype(F32)
     for d in range(128):
-        out_ref[d, 128:SENT, :] = jnp.where(
-            row == 0, high[d : d + 1, :], jnp.where(row == 1, low[d : d + 1, :], 0.0)
-        ).astype(BF16)
-    low = lax.broadcasted_iota(jnp.int32, (8, LIVE), 0)
+        codes = jnp.where(row == 0, high[d : d + 1, :], jnp.where(row == 1, low[d : d + 1, :], 0.0))
+        out_ref[d] = jnp.concatenate([jnp.zeros((128, 128), F32), codes], axis=0).astype(BF16)
+    low = lax.broadcasted_iota(jnp.int32, (16, LIVE), 0)
+    zero = jnp.zeros((), BF16)
 
     def block(b, c):
         _, share, _ = depth_parts(first_ref, count_ref, weight_ref, b)
@@ -123,16 +118,21 @@
         for chunk in range(4):
 
             def quad(i, acc):
+                mine, high = [], []
                 for step in range(4):
                     d = jnp.minimum(first + 4 * i + step, BINS - 1)
-                    slot = jnp.broadcast_to(slot_ref[b, pl.ds(d, 1), :], (8, LIVE))
-                    share = jnp.broadcast_to(prob[pl.ds(d, 1), :], (8, LIVE))
-                    mine = jnp.where((slot & 7) == low, share, 0.0)
-                    high = (slot >> 3) - chunk * 32
-                    acc = [a + jnp.where(high == r, mine, 0.0) for r, a in enumerate(acc)]
-                return acc
-
-            acc = lax.fori_loop(0, quads, quad, [jnp.zeros((8, LIVE), F32)] * 32)
+                    slot = jnp.broadcast_to(slot_ref[b, pl.ds(d, 1), :], (16, LIVE))
+                    share = jnp.broadcast_to(prob[pl.ds(d, 1), :], (16, LIVE))
+                    mine.append(jnp.where((slot & 15) == low, share, 0.0).astype(BF16))
+                    high.append(((slot >> 4) - chunk * 16).astype(F32).astype(BF16))
+                new = []
+                for r, a in enumerate(acc):
+                    at = jnp.full((), r, BF16)
+                    hits = [jnp.where(h == at, m, zero) for h, m in zip(high, mine)]
+                    new.append(a + ((hits[0] + hits[1]) + (hits[2] + hits[3])).astype(F32))
+                return new
+
+            acc = lax.fori_loop(0, quads, quad, [jnp.zeros((16, LIVE), F32)] * 16)
             table_ref[b, chunk * 256 : (chunk + 1) * 256, :] = jnp.concatenate(acc, axis=0).astype(
                 BF16
             )
@@ -193,7 +193,7 @@
     first_half = lax.broadcasted_iota(jnp.int32, (1, 128), 1) < 64
     one, zero = jnp.ones((), BF16), jnp.zeros((), BF16)
     for n in range(64):
-        codes = [list_ref[2 * n + e, 128:SENT, :].astype(F32) for e in range(2)]
+        codes = [list_ref[2 * n + e].astype(F32)[128:, :] for e in range(2)]
         for i in range(2):
             code[n // 8 * 2 + i : n // 8 * 2 + i + 1, n % 8 * 128 : n % 8 * 128 + 128] = jnp.where(
                 first_half, codes[0][i : i + 1, :], codes[1][i : i + 1, :]
@@ -398,8 +398,9 @@
     spread(flat, wide)
     lay_out(flat2, gout_ref, *rims, 1)
     spread(flat2, gwide)
-    flat[...] = jnp.zeros_like(flat)
-    flat2[...] = jnp.zeros_like(flat2)
+    for values in (flat, flat2):
+        values[: WIDE0 + 8, :] = jnp.zeros((WIDE0 + 8, CH), F32)
+        values[WIDE0 + 8 + WIDE :, :] = jnp.zeros((FLAT + 8 - WIDE0 - WIDE, CH), F32)
     for load in loads:
         load.wait()
 

time: 268 us -> 263 us (0.981)
  waiting for transfers between devices: 126 us -> 123 us
    all_to_all x3, waiting for transfers between devices: 118 us -> 115 us  [exchanged(): lax.all_to_all(values, ('by', 'bx'), split_axis=0, concat_axis=0, tiled=T...]
where the time goes in v2:
time: 263 us; the launch traced here: 262 us
  waiting for transfers between devices  123 us (47%)
  Pallas kernels  84.1 us (32%)
  starting transfers between devices  36.4 us (14%)
  local copies, waits for them, and re-layouts  14.2 us (5%)
  other arithmetic  2.95 us (1%)
    all_to_all x3, waiting for transfers between devices, exchanged(): lax.all_to_all(values, ('by', 'bx'), split_axis=0, concat_axis=0, tiled=T...  115 us
    all_to_all x3, starting transfers between devices, exchanged(): lax.all_to_all(values, ('by', 'bx'), split_axis=0, concat_axis=0, tiled=T...  27.9 us
    pallas_call x1, Pallas kernels, send_back(): call(back_kernel, [VMEM] * 3, jax.ShapeDtypeStruct((128, BACK, 128), BF16...  20.2 us
    pallas_call x1, Pallas kernels, activate_tile(): call(act_kernel, [SMEM, ANY, ANY] + [VMEM] * 6, (flat, flat, jax.ShapeDty...  18.2 us
    pallas_call x1, Pallas kernels, lift(): call(lift_kernel, [SMEM] * 4 + [VMEM] * 4, (jax.ShapeDtypeStruct((128, SE...  11.9 us
    pallas_call x1, Pallas kernels, splat(): call(splat_kernel, [VMEM] * 2, (jax.ShapeDtypeStruct((CELLS, CH), BF16),)...  11.1 us
    ppermute x4, starting transfers between devices, shifted(): lax.ppermute(values, axis, [(i, i + step) for i in range(count) if 0 <= i...  7.52 us
    ppermute x4, waiting for transfers between devices, shifted(): lax.ppermute(values, axis, [(i, i + step) for i in range(count) if 0 <= i...  7.5 us
  transfers between devices with their start and end apart: 8, of which 5 were waited for; matrix products, arithmetic and copies ran while one was open for 4% of the time, Pallas kernels for 14%

profile of v2, /device:TPU:1, one launch (start us, length us, event | category | flops | bytes accessed | tf_op | source)
XLA Modules:
  0.0 261.6 jit_solution(5116975946802014003)
XLA Ops:
  0.6 11.9 %shard_map.146 = (bf16[128,136,128]{2,1,0:T(8,128)(2,1)}, bf16[4,1024,128]{2,1,0:T(8,128)(2,1)}, s32[128]{0:T(128)}) custom-call(s32[4]{0:T(128)} %first_ref.3, s32[4]{0:T(128)} %count_ref.3, s32[4]{0:T(128)} %live_ref.3, s32[4,32]{1,0:T(4,128)} %dest_ref.1, bf16[4,128,256]{2,1,0:T(8,128)(2,1)} %feat_ref.3, f32[4,64,128]{2,1,0:T(8,128)} %weight_ref.3, ...), custom_call_target="tpu_custom_call" | custom-call | flops 300000000 | bytes 6000000 | tf_op jit(solution)/shard_map/pallas_call | solution.py:155
  12.5 12.5 %all-to-all-start = ((bf16[128,136,128]{2,1,0:T(8,128)(2,1)}), bf16[128,136,128]{2,1,0:T(8,128)(2,1)}, u32[]{:S(2)}, u32[]{:S(2)}) async-start(bf16[128,136,128]{2,1,0:T(8,128)(2,1)} %get-tuple-element.37), calls=%async_computation | async-start | bytes 8912896 | tf_op jit(solution)/shard_map/all_to_all | solution.py:660
  25.1 1.3 copy.17
  27.5 3.4 %shard_map.147 = (bf16[2304,256]{1,0:T(8,128)(2,1)}, bf16[2304,256]{1,0:T(8,128)(2,1)}) custom-call(bf16[2304,256]{1,0:T(8,128)(2,1)} %bitcast.20, bf16[2304,256]{1,0:T(8,128)(2,1)} %bitcast.22), custom_call_target="tpu_custom_call" | custom-call | flops 10000000 | bytes 5000000 | tf_op jit(solution)/shard_map/pallas_call | solution.py:333
  32.4 48.3 %all-to-all-done.list_ref = bf16[128,136,128]{2,1,0:T(8,128)(2,1)} async-done(((bf16[128,136,128]{2,1,0:T(8,128)(2,1)}), bf16[128,136,128]{2,1,0:T(8,128)(2,1)}, u32[]{:S(2)}, u32[]{:S(2)}) %all-to-all-start) | async-done | bytes 4456480 | tf_op jit(solution)/shard_map/all_to_all | solution.py:660
  80.7 11.1 %shard_map.148 = (bf16[1600,256]{1,0:T(8,128)(2,1)}, bf16[160,256]{1,0:T(8,128)(2,1)}, bf16[160,256]{1,0:T(8,128)(2,1)}, bf16[160,256]{1,0:T(8,128)(2,1)}, bf16[160,256]{1,0:T(8,128)(2,1)}) custom-call(bf16[128,136,128]{2,1,0:T(8,128)(2,1)} %all-to-all-done.list_ref, bf16[4,80,256]{2,1,0:T(8,128)(2,1)} %pad_maximum_fusion.gout_ref), custom_call_target="tpu_custom_call" | custom-call | flops 6700000256 | bytes 6000000 | tf_op jit(solution)/shard_map/pallas_call | solution.py:239
  91.8 2.8 %collective-permute-start = (bf16[160,256]{1,0:T(8,128)(2,1)}, bf16[160,256]{1,0:T(8,128)(2,1)S(1)}, u32[]{:S(2)}, u32[]{:S(2)}) collective-permute-start(bf16[160,256]{1,0:T(8,128)(2,1)} %get-tuple-element.50), channel_id=1, source_target_pairs={{0,1},{1,2},{2,3},{3,4},{4,5},{5,6},{6,7},{8,9},{9,10},{10,11},{11... | collective-permute-start | bytes 245768 | tf_op jit(solution)/shard_map/ppermute | solution.py:276
  94.7 1.9 collective-permute-start.1
  96.6 4.0 %collective-permute-done.1.right_ref = bf16[160,256]{1,0:T(8,128)(2,1)S(1)} collective-permute-done((bf16[160,256]{1,0:T(8,128)(2,1)}, bf16[160,256]{1,0:T(8,128)(2,1)S(1)}, u32[]{:S(2)}, u32[]{:S(2)}) %collective-permute-start.1) | collective-permute-done | bytes 81952 | tf_op jit(solution)/shard_map/ppermute | solution.py:276
  101.3 1.7 shard_map.149
  104.3 1.5 collective-permute-start.3
  106.4 3.5 %collective-permute-done.3.below_ref = bf16[192,256]{1,0:T(8,128)(2,1)S(1)} collective-permute-done((bf16[192,256]{1,0:T(8,128)(2,1)}, bf16[192,256]{1,0:T(8,128)(2,1)S(1)}, u32[]{:S(2)}, u32[]{:S(2)}) %collective-permute-start.3) | collective-permute-done | bytes 98336 | tf_op jit(solution)/shard_map/ppermute | solution.py:276
  110.5 18.2 %shard_map.150 = (bf16[2160,256]{1,0:T(8,128)(2,1)}, bf16[2160,256]{1,0:T(8,128)(2,1)}, bf16[2,4608,128]{2,1,0:T(8,128)(2,1)}) custom-call(s32[2]{0:T(128)} %pad_add_fusion.spot_ref, bf16[2304,256]{1,0:T(8,128)(2,1)} %bitcast.21, bf16[2304,256]{1,0:T(8,128)(2,1)} %get-tuple-element.45.second_hbm, bf16[1600,256]{1,0:T(8,128)(2,1)} %get-tuple-element.47.base_ref, ...), custom_call_target="tpu_custom_call" | custom-call | flops 8999999488 | bytes 9000000 | tf_op jit(solution)/shard_map/pallas_call | solution.py:431
  128.7 9.9 %all-to-all-start.1 = ((bf16[128,72,128]{2,1,0:T(8,128)(2,1)}), bf16[128,72,128]{2,1,0:T(8,128)(2,1)S(1)}, u32[]{:S(2)}, u32[]{:S(2)}) async-start(bf16[128,72,128]{2,1,0:T(8,128)(2,1)} %bitcast.19), calls=%async_computation.1 | async-start | bytes 4718592 | tf_op jit(solution)/shard_map/all_to_all | solution.py:660
  139.9 5.6 %convert_element_type.24.cell_ref = s32[8192,1]{1,0:T(8,128)} reshape(s32[128,64]{1,0:T(8,128)S(1)} %fusion.1) | data formatting | bytes 65536 | tf_op jit(solution)/shard_map/convert_element_type | solution.py:720
  145.6 20.2 %shard_map.151 = bf16[128,168,128]{2,1,0:T(8,128)(2,1)} custom-call(bf16[2304,256]{1,0:T(8,128)(2,1)} %get-tuple-element.43.first_ref, s32[8192,1]{1,0:T(8,128)} %convert_element_type.24.cell_ref, bf16[2160,256]{1,0:T(8,128)(2,1)} %get-tuple-element.56.fcot_ref), custom_call_target="tpu_custom_call" | custom-call | flops 8999999488 | bytes 12000000 | tf_op jit(solution)/shard_map/pallas_call | solution.py:498
  165.8 6.2 %all-to-all-done.1 = bf16[128,72,128]{2,1,0:T(8,128)(2,1)S(1)} async-done(((bf16[128,72,128]{2,1,0:T(8,128)(2,1)}), bf16[128,72,128]{2,1,0:T(8,128)(2,1)S(1)}, u32[]{:S(2)}, u32[]{:S(2)}) %all-to-all-start.1) | async-done | bytes 2359328 | tf_op jit(solution)/shard_map/all_to_all | solution.py:660
  172.5 1.4 constant_dynamic-update-slice_fusion
  173.9 5.5 %all-to-all-start.2 = ((bf16[128,168,128]{2,1,0:T(8,128)(2,1)}), bf16[128,168,128]{2,1,0:T(8,128)(2,1)}, u32[]{:S(2)}, u32[]{:S(2)}) async-start(bf16[128,168,128]{2,1,0:T(8,128)(2,1)} %constant_dynamic-update-slice_fusion), calls=%async_computation.2 | async-start | bytes 11010048 | tf_op jit(solution)/shard_map/all_to_all | solution.py:660
  179.4 6.1 %shard_map.152 = bf16[1600,256]{1,0:T(8,128)(2,1)} custom-call(bf16[2304,256]{1,0:T(8,128)(2,1)} %bitcast.23, bf16[2160,256]{1,0:T(8,128)(2,1)} %get-tuple-element.58.hidden_ref), custom_call_target="tpu_custom_call" | custom-call | flops 2300000000 | bytes 5000000 | tf_op jit(solution)/shard_map/pallas_call | solution.py:532
  185.6 60.9 %all-to-all-done.2.back_ref = bf16[128,168,128]{2,1,0:T(8,128)(2,1)} async-done(((bf16[128,168,128]{2,1,0:T(8,128)(2,1)}), bf16[128,168,128]{2,1,0:T(8,128)(2,1)}, u32[]{:S(2)}, u32[]{:S(2)}) %all-to-all-start.2) | async-done | bytes 5505056 | tf_op jit(solution)/shard_map/all_to_all | solution.py:660
  246.5 1.4 slice.41.own_ref
  248.9 7.4 %shard_map.153 = (bf16[4,128,256]{2,1,0:T(8,128)(2,1)}, f32[4,64,128]{2,1,0:T(8,128)}) custom-call(s32[4]{0:T(128)} %first_ref.3, s32[4]{0:T(128)} %count_ref.3, s32[4]{0:T(128)} %live_ref.3, s32[128]{0:T(128)} %get-tuple-element.60.route_ref, bf16[4,128,256]{2,1,0:T(8,128)(2,1)} %feat_ref.3, f32[4,64,128]{2,1,0:T(8,128)} %weight_ref.3, ...), custom_call_target="tpu_custom_call" | custom-call | flops 600000000 | bytes 8000000 | tf_op jit(solution)/shard_map/pallas_call | solution.py:641
  257.3 4.1 %shard_map.154 = (f32[9,256,256]{2,1,0:T(8,128)}, f32[9,256,256]{2,1,0:T(8,128)}) custom-call(s32[2]{0:T(128)} %pad_add_fusion.spot_ref, bf16[128,40,128]{2,1,0:T(8,128)(2,1)} %copy-done, bf16[128,40,128]{2,1,0:T(8,128)(2,1)} %copy-done.1), custom_call_target="tpu_custom_call" | custom-call | flops 1000000 | bytes 7000000 | tf_op jit(solution)/shard_map/pallas_call | solution.py:571
  (31 shorter events, 9.6 us)
Async XLA Ops:
  12.5 12.5 %copy-start.2 = (bf16[4,1024,128]{2,1,0:T(8,128)(2,1)S(1)}, bf16[4,1024,128]{2,1,0:T(8,128)(2,1)}, u32[]{:S(2)}) copy-start(bf16[4,1024,128]{2,1,0:T(8,128)(2,1)} %get-tuple-element.38) | copy-start | bytes 3145732
  12.5 68.2 %all-to-all-start = ((bf16[128,136,128]{2,1,0:T(8,128)(2,1)}), bf16[128,136,128]{2,1,0:T(8,128)(2,1)}, u32[]{:S(2)}, u32[]{:S(2)}) async-start(bf16[128,136,128]{2,1,0:T(8,128)(2,1)} %get-tuple-element.37), calls=%async_computation | async-start | bytes 8912896 | tf_op jit(solution)/shard_map/all_to_all | solution.py:660
  91.8 4.8 %collective-permute-start = (bf16[160,256]{1,0:T(8,128)(2,1)}, bf16[160,256]{1,0:T(8,128)(2,1)S(1)}, u32[]{:S(2)}, u32[]{:S(2)}) collective-permute-start(bf16[160,256]{1,0:T(8,128)(2,1)} %get-tuple-element.50), channel_id=1, source_target_pairs={{0,1},{1,2},{2,3},{3,4},{4,5},{5,6},{6,7},{8,9},{9,10},{10,11},{11... | collective-permute-start | bytes 245768 | tf_op jit(solution)/shard_map/ppermute | solution.py:276
  94.7 6.0 %collective-permute-start.1 = (bf16[160,256]{1,0:T(8,128)(2,1)}, bf16[160,256]{1,0:T(8,128)(2,1)S(1)}, u32[]{:S(2)}, u32[]{:S(2)}) collective-permute-start(bf16[160,256]{1,0:T(8,128)(2,1)} %get-tuple-element.51), channel_id=1, source_target_pairs={{1,0},{2,1},{3,2},{4,3},{5,4},{6,5},{7,6},{9,8},{10,9},{11,10},{12... | collective-permute-start | bytes 245768 | tf_op jit(solution)/shard_map/ppermute | solution.py:276
  96.6 4.0 %copy-start.3 = (bf16[160,256]{1,0:T(8,128)(2,1)}, bf16[160,256]{1,0:T(8,128)(2,1)S(1)}, u32[]{:S(2)}) copy-start(bf16[160,256]{1,0:T(8,128)(2,1)S(1)} %collective-permute-done.left_ref) | copy-start | bytes 245764
  100.7 0.6 copy-start.4
  103.0 3.4 %collective-permute-start.2 = (bf16[192,256]{1,0:T(8,128)(2,1)}, bf16[192,256]{1,0:T(8,128)(2,1)S(1)}, u32[]{:S(2)}, u32[]{:S(2)}) collective-permute-start(bf16[192,256]{1,0:T(8,128)(2,1)} %get-tuple-element.52), channel_id=1, source_target_pairs={{0,8},{8,16},{16,24},{24,32},{32,40},{40,48},{48,56},{56,64},{64,7... | collective-permute-start | bytes 294920 | tf_op jit(solution)/shard_map/ppermute | solution.py:276
  104.3 5.6 %collective-permute-start.3 = (bf16[192,256]{1,0:T(8,128)(2,1)}, bf16[192,256]{1,0:T(8,128)(2,1)S(1)}, u32[]{:S(2)}, u32[]{:S(2)}) collective-permute-start(bf16[192,256]{1,0:T(8,128)(2,1)} %get-tuple-element.53), channel_id=1, source_target_pairs={{8,0},{16,8},{24,16},{32,24},{40,32},{48,40},{56,48},{64,56},{72,6... | collective-permute-start | bytes 294920 | tf_op jit(solution)/shard_map/ppermute | solution.py:276
  106.4 3.5 %copy-start.5 = (bf16[192,256]{1,0:T(8,128)(2,1)}, bf16[192,256]{1,0:T(8,128)(2,1)S(1)}, u32[]{:S(2)}) copy-start(bf16[192,256]{1,0:T(8,128)(2,1)S(1)} %collective-permute-done.2.above_ref) | copy-start | bytes 294916
  109.8 0.6 copy-start.6
  128.7 43.3 %all-to-all-start.1 = ((bf16[128,72,128]{2,1,0:T(8,128)(2,1)}), bf16[128,72,128]{2,1,0:T(8,128)(2,1)S(1)}, u32[]{:S(2)}, u32[]{:S(2)}) async-start(bf16[128,72,128]{2,1,0:T(8,128)(2,1)} %bitcast.19), calls=%async_computation.1 | async-start | bytes 4718592 | tf_op jit(solution)/shard_map/all_to_all | solution.py:660
  173.9 72.6 %all-to-all-start.2 = ((bf16[128,168,128]{2,1,0:T(8,128)(2,1)}), bf16[128,168,128]{2,1,0:T(8,128)(2,1)}, u32[]{:S(2)}, u32[]{:S(2)}) async-start(bf16[128,168,128]{2,1,0:T(8,128)(2,1)} %constant_dynamic-update-slice_fusion), calls=%async_computation.2 | async-start | bytes 11010048 | tf_op jit(solution)/shard_map/all_to_all | solution.py:660
  247.9 8.3 %copy-start = (bf16[128,40,128]{2,1,0:T(8,128)(2,1)}, bf16[128,40,128]{2,1,0:T(8,128)(2,1)S(1)}, u32[]{:S(2)}) copy-start(bf16[128,40,128]{2,1,0:T(8,128)(2,1)S(1)} %slice.41.own_ref) | copy-start | bytes 3932164
  247.9 8.3 %collective-permute-start.4 = (bf16[128,40,128]{2,1,0:T(8,128)(2,1)S(1)}, bf16[128,40,128]{2,1,0:T(8,128)(2,1)S(1)}, u32[]{:S(2)}, u32[]{:S(2)}) collective-permute-start(bf16[128,40,128]{2,1,0:T(8,128)(2,1)S(1)} %slice.41.own_ref), channel_id=1, source_target_pairs={{0,1},{1,0},{2,3},{3,2},{4,5},{5,4},{6,7},{7,6},{8,9},{9,8},{10,11... | collective-permute-start | bytes 3932168 | tf_op jit(solution)/shard_map/ppermute | solution.py:728
  256.3 1.1 copy-start.1

commit v3 on v2

--- a/solution.py
+++ b/solution.py
@@ -405,18 +405,18 @@
         load.wait()
 
     def activate(k, c):
-        at = pl.multiple_of(WIDE0 + k * 512, 16)
-        first_act = taps(wide, first_ref, at, 512)
-        hidden_cot = taps(gwide, second_ref, at, 512)
-        inside = place_mask(spot_ref[0], spot_ref[1], at, 512, 1)
+        at = pl.multiple_of(WIDE0 + k * 1024, 16)
+        first_act = taps(wide, first_ref, at, 1024)
+        hidden_cot = taps(gwide, second_ref, at, 1024)
+        inside = place_mask(spot_ref[0], spot_ref[1], at, 1024, 1)
         sig = jax.nn.sigmoid(first_act)
-        to = pl.ds(pl.multiple_of(at + 8, 8), 512)
+        to = pl.ds(pl.multiple_of(at + 8, 8), 1024)
         flat2[to, :] = jnp.where(inside, first_act * sig, 0.0)
         slope = sig * (1.0 + first_act * (1.0 - sig))
         flat[to, :] = jnp.where(inside, hidden_cot * slope, 0.0)
         return c
 
-    lax.fori_loop(0, WIDE // 512, activate, 0)
+    lax.fori_loop(0, WIDE // 1024, activate, 0)
     fcot_ref[...] = flat[8 : 8 + FLAT, :].astype(BF16)
     hidden_ref[...] = flat2[8 : 8 + FLAT, :].astype(BF16)
     turn(spot_ref, lambda at: flat[at + 8 : at + 264, :], turned)
@@ -627,7 +627,9 @@
                     acc = jnp.where(high == row, found, acc)
                 return acc
 
-            pick[pl.ds(at, 8), :] = lax.fori_loop(0, 8, group, jnp.zeros((8, LIVE), F32))
+            pick[pl.ds(at, 8), :] = lax.fori_loop(
+                0, 8, group, jnp.zeros((8, LIVE), F32), unroll=True
+            )
             return c
 
         lax.fori_loop(first >> 3, (first + count_ref[b] + 7) >> 3, eight, 0)

time: 263 us -> 261 us (level)
  no operation moved by 1% of the time
where the time goes in v3:
time: 261 us
  waiting for transfers between devices  123 us (47%)
  Pallas kernels  83.3 us (32%)
  starting transfers between devices  36.4 us (14%)
  local copies, waits for them, and re-layouts  14.2 us (5%)
  other arithmetic  2.95 us (1%)
    all_to_all x3, waiting for transfers between devices, exchanged(): lax.all_to_all(values, ('by', 'bx'), split_axis=0, concat_axis=0, tiled=T...  115 us
    all_to_all x3, starting transfers between devices, exchanged(): lax.all_to_all(values, ('by', 'bx'), split_axis=0, concat_axis=0, tiled=T...  28 us
    pallas_call x1, Pallas kernels, send_back(): call(back_kernel, [VMEM] * 3, jax.ShapeDtypeStruct((128, BACK, 128), BF16...  20.2 us
    pallas_call x1, Pallas kernels, activate_tile(): call(act_kernel, [SMEM, ANY, ANY] + [VMEM] * 6, (flat, flat, jax.ShapeDty...  18 us
    pallas_call x1, Pallas kernels, lift(): call(lift_kernel, [SMEM] * 4 + [VMEM] * 4, (jax.ShapeDtypeStruct((128, SE...  11.9 us
    pallas_call x1, Pallas kernels, splat(): call(splat_kernel, [VMEM] * 2, (jax.ShapeDtypeStruct((CELLS, CH), BF16),)...  11.1 us
    ppermute x4, starting transfers between devices, shifted(): lax.ppermute(values, axis, [(i, i + step) for i in range(count) if 0 <= i...  7.51 us
    ppermute x4, waiting for transfers between devices, shifted(): lax.ppermute(values, axis, [(i, i + step) for i in range(count) if 0 <= i...  7.5 us
  transfers between devices with their start and end apart: 8, of which 5 were waited for; matrix products, arithmetic and copies ran while one was open for 4% of the time, Pallas kernels for 14%

profile of v3, /device:TPU:1, one launch (start us, length us, event | category | flops | bytes accessed | tf_op | source)
XLA Modules:
  0.0 260.8 jit_solution(2931096395105146213)
XLA Ops:
  0.6 11.9 %shard_map.146 = (bf16[128,136,128]{2,1,0:T(8,128)(2,1)}, bf16[4,1024,128]{2,1,0:T(8,128)(2,1)}, s32[128]{0:T(128)}) custom-call(s32[4]{0:T(128)} %first_ref.3, s32[4]{0:T(128)} %count_ref.3, s32[4]{0:T(128)} %live_ref.3, s32[4,32]{1,0:T(4,128)} %dest_ref.1, bf16[4,128,256]{2,1,0:T(8,128)(2,1)} %feat_ref.3, f32[4,64,128]{2,1,0:T(8,128)} %weight_ref.3, ...), custom_call_target="tpu_custom_call" | custom-call | flops 300000000 | bytes 6000000 | tf_op jit(solution)/shard_map/pallas_call | solution.py:155
  12.5 12.5 %all-to-all-start = ((bf16[128,136,128]{2,1,0:T(8,128)(2,1)}), bf16[128,136,128]{2,1,0:T(8,128)(2,1)}, u32[]{:S(2)}, u32[]{:S(2)}) async-start(bf16[128,136,128]{2,1,0:T(8,128)(2,1)} %get-tuple-element.37), calls=%async_computation | async-start | bytes 8912896 | tf_op jit(solution)/shard_map/all_to_all | solution.py:662
  25.1 1.3 copy.17
  27.5 3.4 %shard_map.147 = (bf16[2304,256]{1,0:T(8,128)(2,1)}, bf16[2304,256]{1,0:T(8,128)(2,1)}) custom-call(bf16[2304,256]{1,0:T(8,128)(2,1)} %bitcast.20, bf16[2304,256]{1,0:T(8,128)(2,1)} %bitcast.22), custom_call_target="tpu_custom_call" | custom-call | flops 10000000 | bytes 5000000 | tf_op jit(solution)/shard_map/pallas_call | solution.py:333
  32.4 48.3 %all-to-all-done.list_ref = bf16[128,136,128]{2,1,0:T(8,128)(2,1)} async-done(((bf16[128,136,128]{2,1,0:T(8,128)(2,1)}), bf16[128,136,128]{2,1,0:T(8,128)(2,1)}, u32[]{:S(2)}, u32[]{:S(2)}) %all-to-all-start) | async-done | bytes 4456480 | tf_op jit(solution)/shard_map/all_to_all | solution.py:662
  80.8 11.1 %shard_map.148 = (bf16[1600,256]{1,0:T(8,128)(2,1)}, bf16[160,256]{1,0:T(8,128)(2,1)}, bf16[160,256]{1,0:T(8,128)(2,1)}, bf16[160,256]{1,0:T(8,128)(2,1)}, bf16[160,256]{1,0:T(8,128)(2,1)}) custom-call(bf16[128,136,128]{2,1,0:T(8,128)(2,1)} %all-to-all-done.list_ref, bf16[4,80,256]{2,1,0:T(8,128)(2,1)} %pad_maximum_fusion.gout_ref), custom_call_target="tpu_custom_call" | custom-call | flops 6700000256 | bytes 6000000 | tf_op jit(solution)/shard_map/pallas_call | solution.py:239
  91.9 2.8 %collective-permute-start = (bf16[160,256]{1,0:T(8,128)(2,1)}, bf16[160,256]{1,0:T(8,128)(2,1)S(1)}, u32[]{:S(2)}, u32[]{:S(2)}) collective-permute-start(bf16[160,256]{1,0:T(8,128)(2,1)} %get-tuple-element.50), channel_id=1, source_target_pairs={{0,1},{1,2},{2,3},{3,4},{4,5},{5,6},{6,7},{8,9},{9,10},{10,11},{11... | collective-permute-start | bytes 245768 | tf_op jit(solution)/shard_map/ppermute | solution.py:276
  94.7 1.9 collective-permute-start.1
  96.7 4.0 %collective-permute-done.1.right_ref = bf16[160,256]{1,0:T(8,128)(2,1)S(1)} collective-permute-done((bf16[160,256]{1,0:T(8,128)(2,1)}, bf16[160,256]{1,0:T(8,128)(2,1)S(1)}, u32[]{:S(2)}, u32[]{:S(2)}) %collective-permute-start.1) | collective-permute-done | bytes 81952 | tf_op jit(solution)/shard_map/ppermute | solution.py:276
  101.3 1.7 shard_map.149
  104.3 1.5 collective-permute-start.3
  106.4 3.5 %collective-permute-done.3.below_ref = bf16[192,256]{1,0:T(8,128)(2,1)S(1)} collective-permute-done((bf16[192,256]{1,0:T(8,128)(2,1)}, bf16[192,256]{1,0:T(8,128)(2,1)S(1)}, u32[]{:S(2)}, u32[]{:S(2)}) %collective-permute-start.3) | collective-permute-done | bytes 98336 | tf_op jit(solution)/shard_map/ppermute | solution.py:276
  110.5 18.0 %shard_map.150 = (bf16[2160,256]{1,0:T(8,128)(2,1)}, bf16[2160,256]{1,0:T(8,128)(2,1)}, bf16[2,4608,128]{2,1,0:T(8,128)(2,1)}) custom-call(s32[2]{0:T(128)} %pad_add_fusion.spot_ref, bf16[2304,256]{1,0:T(8,128)(2,1)} %bitcast.21, bf16[2304,256]{1,0:T(8,128)(2,1)} %get-tuple-element.45.second_hbm, bf16[1600,256]{1,0:T(8,128)(2,1)} %get-tuple-element.47.base_ref, ...), custom_call_target="tpu_custom_call" | custom-call | flops 8999999488 | bytes 9000000 | tf_op jit(solution)/shard_map/pallas_call | solution.py:431
  128.5 9.9 %all-to-all-start.1 = ((bf16[128,72,128]{2,1,0:T(8,128)(2,1)}), bf16[128,72,128]{2,1,0:T(8,128)(2,1)S(1)}, u32[]{:S(2)}, u32[]{:S(2)}) async-start(bf16[128,72,128]{2,1,0:T(8,128)(2,1)} %bitcast.19), calls=%async_computation.1 | async-start | bytes 4718592 | tf_op jit(solution)/shard_map/all_to_all | solution.py:662
  139.7 5.6 %convert_element_type.24.cell_ref = s32[8192,1]{1,0:T(8,128)} reshape(s32[128,64]{1,0:T(8,128)S(1)} %fusion.1) | data formatting | bytes 65536 | tf_op jit(solution)/shard_map/convert_element_type | solution.py:722
  145.4 20.2 %shard_map.151 = bf16[128,168,128]{2,1,0:T(8,128)(2,1)} custom-call(bf16[2304,256]{1,0:T(8,128)(2,1)} %get-tuple-element.43.first_ref, s32[8192,1]{1,0:T(8,128)} %convert_element_type.24.cell_ref, bf16[2160,256]{1,0:T(8,128)(2,1)} %get-tuple-element.56.fcot_ref), custom_call_target="tpu_custom_call" | custom-call | flops 8999999488 | bytes 12000000 | tf_op jit(solution)/shard_map/pallas_call | solution.py:498
  165.6 6.2 %all-to-all-done.1 = bf16[128,72,128]{2,1,0:T(8,128)(2,1)S(1)} async-done(((bf16[128,72,128]{2,1,0:T(8,128)(2,1)}), bf16[128,72,128]{2,1,0:T(8,128)(2,1)S(1)}, u32[]{:S(2)}, u32[]{:S(2)}) %all-to-all-start.1) | async-done | bytes 2359328 | tf_op jit(solution)/shard_map/all_to_all | solution.py:662
  172.3 1.4 constant_dynamic-update-slice_fusion
  173.7 5.5 %all-to-all-start.2 = ((bf16[128,168,128]{2,1,0:T(8,128)(2,1)}), bf16[128,168,128]{2,1,0:T(8,128)(2,1)}, u32[]{:S(2)}, u32[]{:S(2)}) async-start(bf16[128,168,128]{2,1,0:T(8,128)(2,1)} %constant_dynamic-update-slice_fusion), calls=%async_computation.2 | async-start | bytes 11010048 | tf_op jit(solution)/shard_map/all_to_all | solution.py:662
  179.2 6.1 %shard_map.152 = bf16[1600,256]{1,0:T(8,128)(2,1)} custom-call(bf16[2304,256]{1,0:T(8,128)(2,1)} %bitcast.23, bf16[2160,256]{1,0:T(8,128)(2,1)} %get-tuple-element.58.hidden_ref), custom_call_target="tpu_custom_call" | custom-call | flops 2300000000 | bytes 5000000 | tf_op jit(solution)/shard_map/pallas_call | solution.py:532
  185.4 60.9 %all-to-all-done.2.back_ref = bf16[128,168,128]{2,1,0:T(8,128)(2,1)} async-done(((bf16[128,168,128]{2,1,0:T(8,128)(2,1)}), bf16[128,168,128]{2,1,0:T(8,128)(2,1)}, u32[]{:S(2)}, u32[]{:S(2)}) %all-to-all-start.2) | async-done | bytes 5505056 | tf_op jit(solution)/shard_map/all_to_all | solution.py:662
  246.3 1.4 slice.41.own_ref
  248.7 6.8 %shard_map.153 = (bf16[4,128,256]{2,1,0:T(8,128)(2,1)}, f32[4,64,128]{2,1,0:T(8,128)}) custom-call(s32[4]{0:T(128)} %first_ref.3, s32[4]{0:T(128)} %count_ref.3, s32[4]{0:T(128)} %live_ref.3, s32[128]{0:T(128)} %get-tuple-element.60.route_ref, bf16[4,128,256]{2,1,0:T(8,128)(2,1)} %feat_ref.3, f32[4,64,128]{2,1,0:T(8,128)} %weight_ref.3, ...), custom_call_target="tpu_custom_call" | custom-call | flops 600000000 | bytes 8000000 | tf_op jit(solution)/shard_map/pallas_call | solution.py:643
  256.5 4.1 %shard_map.154 = (f32[9,256,256]{2,1,0:T(8,128)}, f32[9,256,256]{2,1,0:T(8,128)}) custom-call(s32[2]{0:T(128)} %pad_add_fusion.spot_ref, bf16[128,40,128]{2,1,0:T(8,128)(2,1)} %copy-done, bf16[128,40,128]{2,1,0:T(8,128)(2,1)} %copy-done.1), custom_call_target="tpu_custom_call" | custom-call | flops 1000000 | bytes 7000000 | tf_op jit(solution)/shard_map/pallas_call | solution.py:571
  (31 shorter events, 9.6 us)
Async XLA Ops:
  12.5 12.6 %copy-start.2 = (bf16[4,1024,128]{2,1,0:T(8,128)(2,1)S(1)}, bf16[4,1024,128]{2,1,0:T(8,128)(2,1)}, u32[]{:S(2)}) copy-start(bf16[4,1024,128]{2,1,0:T(8,128)(2,1)} %get-tuple-element.38) | copy-start | bytes 3145732
  12.5 68.2 %all-to-all-start = ((bf16[128,136,128]{2,1,0:T(8,128)(2,1)}), bf16[128,136,128]{2,1,0:T(8,128)(2,1)}, u32[]{:S(2)}, u32[]{:S(2)}) async-start(bf16[128,136,128]{2,1,0:T(8,128)(2,1)} %get-tuple-element.37), calls=%async_computation | async-start | bytes 8912896 | tf_op jit(solution)/shard_map/all_to_all | solution.py:662
  91.9 4.8 %collective-permute-start = (bf16[160,256]{1,0:T(8,128)(2,1)}, bf16[160,256]{1,0:T(8,128)(2,1)S(1)}, u32[]{:S(2)}, u32[]{:S(2)}) collective-permute-start(bf16[160,256]{1,0:T(8,128)(2,1)} %get-tuple-element.50), channel_id=1, source_target_pairs={{0,1},{1,2},{2,3},{3,4},{4,5},{5,6},{6,7},{8,9},{9,10},{10,11},{11... | collective-permute-start | bytes 245768 | tf_op jit(solution)/shard_map/ppermute | solution.py:276
  94.7 6.0 %collective-permute-start.1 = (bf16[160,256]{1,0:T(8,128)(2,1)}, bf16[160,256]{1,0:T(8,128)(2,1)S(1)}, u32[]{:S(2)}, u32[]{:S(2)}) collective-permute-start(bf16[160,256]{1,0:T(8,128)(2,1)} %get-tuple-element.51), channel_id=1, source_target_pairs={{1,0},{2,1},{3,2},{4,3},{5,4},{6,5},{7,6},{9,8},{10,9},{11,10},{12... | collective-permute-start | bytes 245768 | tf_op jit(solution)/shard_map/ppermute | solution.py:276
  96.7 4.0 %copy-start.3 = (bf16[160,256]{1,0:T(8,128)(2,1)}, bf16[160,256]{1,0:T(8,128)(2,1)S(1)}, u32[]{:S(2)}) copy-start(bf16[160,256]{1,0:T(8,128)(2,1)S(1)} %collective-permute-done.left_ref) | copy-start | bytes 245764
  100.7 0.6 copy-start.4
  103.0 3.4 %collective-permute-start.2 = (bf16[192,256]{1,0:T(8,128)(2,1)}, bf16[192,256]{1,0:T(8,128)(2,1)S(1)}, u32[]{:S(2)}, u32[]{:S(2)}) collective-permute-start(bf16[192,256]{1,0:T(8,128)(2,1)} %get-tuple-element.52), channel_id=1, source_target_pairs={{0,8},{8,16},{16,24},{24,32},{32,40},{40,48},{48,56},{56,64},{64,7... | collective-permute-start | bytes 294920 | tf_op jit(solution)/shard_map/ppermute | solution.py:276
  104.3 5.6 %collective-permute-start.3 = (bf16[192,256]{1,0:T(8,128)(2,1)}, bf16[192,256]{1,0:T(8,128)(2,1)S(1)}, u32[]{:S(2)}, u32[]{:S(2)}) collective-permute-start(bf16[192,256]{1,0:T(8,128)(2,1)} %get-tuple-element.53), channel_id=1, source_target_pairs={{8,0},{16,8},{24,16},{32,24},{40,32},{48,40},{56,48},{64,56},{72,6... | collective-permute-start | bytes 294920 | tf_op jit(solution)/shard_map/ppermute | solution.py:276
  106.4 3.5 %copy-start.5 = (bf16[192,256]{1,0:T(8,128)(2,1)}, bf16[192,256]{1,0:T(8,128)(2,1)S(1)}, u32[]{:S(2)}) copy-start(bf16[192,256]{1,0:T(8,128)(2,1)S(1)} %collective-permute-done.2.above_ref) | copy-start | bytes 294916
  109.9 0.6 copy-start.6
  128.5 43.3 %all-to-all-start.1 = ((bf16[128,72,128]{2,1,0:T(8,128)(2,1)}), bf16[128,72,128]{2,1,0:T(8,128)(2,1)S(1)}, u32[]{:S(2)}, u32[]{:S(2)}) async-start(bf16[128,72,128]{2,1,0:T(8,128)(2,1)} %bitcast.19), calls=%async_computation.1 | async-start | bytes 4718592 | tf_op jit(solution)/shard_map/all_to_all | solution.py:662
  173.7 72.6 %all-to-all-start.2 = ((bf16[128,168,128]{2,1,0:T(8,128)(2,1)}), bf16[128,168,128]{2,1,0:T(8,128)(2,1)}, u32[]{:S(2)}, u32[]{:S(2)}) async-start(bf16[128,168,128]{2,1,0:T(8,128)(2,1)} %constant_dynamic-update-slice_fusion), calls=%async_computation.2 | async-start | bytes 11010048 | tf_op jit(solution)/shard_map/all_to_all | solution.py:662
  247.7 7.7 %copy-start = (bf16[128,40,128]{2,1,0:T(8,128)(2,1)}, bf16[128,40,128]{2,1,0:T(8,128)(2,1)S(1)}, u32[]{:S(2)}) copy-start(bf16[128,40,128]{2,1,0:T(8,128)(2,1)S(1)} %slice.41.own_ref) | copy-start | bytes 3932164
  247.8 7.7 %collective-permute-start.4 = (bf16[128,40,128]{2,1,0:T(8,128)(2,1)S(1)}, bf16[128,40,128]{2,1,0:T(8,128)(2,1)S(1)}, u32[]{:S(2)}, u32[]{:S(2)}) collective-permute-start(bf16[128,40,128]{2,1,0:T(8,128)(2,1)S(1)} %slice.41.own_ref), channel_id=1, source_target_pairs={{0,1},{1,0},{2,3},{3,2},{4,5},{5,4},{6,7},{7,6},{8,9},{9,8},{10,11... | collective-permute-start | bytes 3932168 | tf_op jit(solution)/shard_map/ppermute | solution.py:730
  255.5 1.1 copy-start.1

commit v4 on v3

--- a/solution.py
+++ b/solution.py
@@ -148,7 +148,7 @@
                 ]
         return c
 
-    lax.fori_loop(0, BLOCKS, block, 0)
+    lax.fori_loop(0, BLOCKS, block, 0, unroll=True)
 
 
 def lift(first, count, live, dest, features, weights, slots, cells):

time: 261 us -> 262 us (level)
  no operation moved by 1% of the time
where the time goes in v4:
time: 262 us; the launch traced here: 261 us
  waiting for transfers between devices  123 us (47%)
  Pallas kernels  83.7 us (32%)
  starting transfers between devices  36.2 us (14%)
  local copies, waits for them, and re-layouts  14.2 us (5%)
  other arithmetic  2.95 us (1%)
    all_to_all x3, waiting for transfers between devices, exchanged(): lax.all_to_all(values, ('by', 'bx'), split_axis=0, concat_axis=0, tiled=T...  115 us
    all_to_all x3, starting transfers between devices, exchanged(): lax.all_to_all(values, ('by', 'bx'), split_axis=0, concat_axis=0, tiled=T...  27.7 us
    pallas_call x1, Pallas kernels, send_back(): call(back_kernel, [VMEM] * 3, jax.ShapeDtypeStruct((128, BACK, 128), BF16...  20.2 us
    pallas_call x1, Pallas kernels, activate_tile(): call(act_kernel, [SMEM, ANY, ANY] + [VMEM] * 6, (flat, flat, jax.ShapeDty...  18 us
    pallas_call x1, Pallas kernels, lift(): call(lift_kernel, [SMEM] * 4 + [VMEM] * 4, (jax.ShapeDtypeStruct((128, SE...  12.3 us
    pallas_call x1, Pallas kernels, splat(): call(splat_kernel, [VMEM] * 2, (jax.ShapeDtypeStruct((CELLS, CH), BF16),)...  11.1 us
    ppermute x4, starting transfers between devices, shifted(): lax.ppermute(values, axis, [(i, i + step) for i in range(count) if 0 <= i...  7.55 us
    ppermute x4, waiting for transfers between devices, shifted(): lax.ppermute(values, axis, [(i, i + step) for i in range(count) if 0 <= i...  7.46 us
  transfers between devices with their start and end apart: 8, of which 5 were waited for; matrix products, arithmetic and copies ran while one was open for 4% of the time, Pallas kernels for 14%

profile of v4, /device:TPU:1, one launch (start us, length us, event | category | flops | bytes accessed | tf_op | source)
XLA Modules:
  0.0 260.9 jit_solution(5855854797776596421)
XLA Ops:
  0.6 12.3 %shard_map.146 = (bf16[128,136,128]{2,1,0:T(8,128)(2,1)}, bf16[4,1024,128]{2,1,0:T(8,128)(2,1)}, s32[128]{0:T(128)}) custom-call(s32[4]{0:T(128)} %first_ref.3, s32[4]{0:T(128)} %count_ref.3, s32[4]{0:T(128)} %live_ref.3, s32[4,32]{1,0:T(4,128)} %dest_ref.1, bf16[4,128,256]{2,1,0:T(8,128)(2,1)} %feat_ref.3, f32[4,64,128]{2,1,0:T(8,128)} %weight_ref.3, ...), custom_call_target="tpu_custom_call" | custom-call | flops 300000000 | bytes 6000000 | tf_op jit(solution)/shard_map/pallas_call | solution.py:155
  12.9 12.2 %all-to-all-start = ((bf16[128,136,128]{2,1,0:T(8,128)(2,1)}), bf16[128,136,128]{2,1,0:T(8,128)(2,1)}, u32[]{:S(2)}, u32[]{:S(2)}) async-start(bf16[128,136,128]{2,1,0:T(8,128)(2,1)} %get-tuple-element.37), calls=%async_computation | async-start | bytes 8912896 | tf_op jit(solution)/shard_map/all_to_all | solution.py:662
  25.2 1.3 copy.17
  27.6 3.4 %shard_map.147 = (bf16[2304,256]{1,0:T(8,128)(2,1)}, bf16[2304,256]{1,0:T(8,128)(2,1)}) custom-call(bf16[2304,256]{1,0:T(8,128)(2,1)} %bitcast.20, bf16[2304,256]{1,0:T(8,128)(2,1)} %bitcast.22), custom_call_target="tpu_custom_call" | custom-call | flops 10000000 | bytes 5000000 | tf_op jit(solution)/shard_map/pallas_call | solution.py:333
  32.5 48.3 %all-to-all-done.list_ref = bf16[128,136,128]{2,1,0:T(8,128)(2,1)} async-done(((bf16[128,136,128]{2,1,0:T(8,128)(2,1)}), bf16[128,136,128]{2,1,0:T(8,128)(2,1)}, u32[]{:S(2)}, u32[]{:S(2)}) %all-to-all-start) | async-done | bytes 4456480 | tf_op jit(solution)/shard_map/all_to_all | solution.py:662
  80.8 11.1 %shard_map.148 = (bf16[1600,256]{1,0:T(8,128)(2,1)}, bf16[160,256]{1,0:T(8,128)(2,1)}, bf16[160,256]{1,0:T(8,128)(2,1)}, bf16[160,256]{1,0:T(8,128)(2,1)}, bf16[160,256]{1,0:T(8,128)(2,1)}) custom-call(bf16[128,136,128]{2,1,0:T(8,128)(2,1)} %all-to-all-done.list_ref, bf16[4,80,256]{2,1,0:T(8,128)(2,1)} %pad_maximum_fusion.gout_ref), custom_call_target="tpu_custom_call" | custom-call | flops 6700000256 | bytes 6000000 | tf_op jit(solution)/shard_map/pallas_call | solution.py:239
  92.0 2.8 %collective-permute-start = (bf16[160,256]{1,0:T(8,128)(2,1)}, bf16[160,256]{1,0:T(8,128)(2,1)S(1)}, u32[]{:S(2)}, u32[]{:S(2)}) collective-permute-start(bf16[160,256]{1,0:T(8,128)(2,1)} %get-tuple-element.50), channel_id=1, source_target_pairs={{0,1},{1,2},{2,3},{3,4},{4,5},{5,6},{6,7},{8,9},{9,10},{10,11},{11... | collective-permute-start | bytes 245768 | tf_op jit(solution)/shard_map/ppermute | solution.py:276
  94.8 1.9 collective-permute-start.1
  96.8 4.0 %collective-permute-done.1.right_ref = bf16[160,256]{1,0:T(8,128)(2,1)S(1)} collective-permute-done((bf16[160,256]{1,0:T(8,128)(2,1)}, bf16[160,256]{1,0:T(8,128)(2,1)S(1)}, u32[]{:S(2)}, u32[]{:S(2)}) %collective-permute-start.1) | collective-permute-done | bytes 81952 | tf_op jit(solution)/shard_map/ppermute | solution.py:276
  101.4 1.7 shard_map.149
  104.4 1.5 collective-permute-start.3
  106.5 3.4 %collective-permute-done.3.below_ref = bf16[192,256]{1,0:T(8,128)(2,1)S(1)} collective-permute-done((bf16[192,256]{1,0:T(8,128)(2,1)}, bf16[192,256]{1,0:T(8,128)(2,1)S(1)}, u32[]{:S(2)}, u32[]{:S(2)}) %collective-permute-start.3) | collective-permute-done | bytes 98336 | tf_op jit(solution)/shard_map/ppermute | solution.py:276
  110.6 18.0 %shard_map.150 = (bf16[2160,256]{1,0:T(8,128)(2,1)}, bf16[2160,256]{1,0:T(8,128)(2,1)}, bf16[2,4608,128]{2,1,0:T(8,128)(2,1)}) custom-call(s32[2]{0:T(128)} %pad_add_fusion.spot_ref, bf16[2304,256]{1,0:T(8,128)(2,1)} %bitcast.21, bf16[2304,256]{1,0:T(8,128)(2,1)} %get-tuple-element.45.second_hbm, bf16[1600,256]{1,0:T(8,128)(2,1)} %get-tuple-element.47.base_ref, ...), custom_call_target="tpu_custom_call" | custom-call | flops 8999999488 | bytes 9000000 | tf_op jit(solution)/shard_map/pallas_call | solution.py:431
  128.6 10.0 %all-to-all-start.1 = ((bf16[128,72,128]{2,1,0:T(8,128)(2,1)}), bf16[128,72,128]{2,1,0:T(8,128)(2,1)S(1)}, u32[]{:S(2)}, u32[]{:S(2)}) async-start(bf16[128,72,128]{2,1,0:T(8,128)(2,1)} %bitcast.19), calls=%async_computation.1 | async-start | bytes 4718592 | tf_op jit(solution)/shard_map/all_to_all | solution.py:662
  139.8 5.6 %convert_element_type.24.cell_ref = s32[8192,1]{1,0:T(8,128)} reshape(s32[128,64]{1,0:T(8,128)S(1)} %fusion.1) | data formatting | bytes 65536 | tf_op jit(solution)/shard_map/convert_element_type | solution.py:722
  145.5 20.2 %shard_map.151 = bf16[128,168,128]{2,1,0:T(8,128)(2,1)} custom-call(bf16[2304,256]{1,0:T(8,128)(2,1)} %get-tuple-element.43.first_ref, s32[8192,1]{1,0:T(8,128)} %convert_element_type.24.cell_ref, bf16[2160,256]{1,0:T(8,128)(2,1)} %get-tuple-element.56.fcot_ref), custom_call_target="tpu_custom_call" | custom-call | flops 8999999488 | bytes 12000000 | tf_op jit(solution)/shard_map/pallas_call | solution.py:498
  165.7 6.2 %all-to-all-done.1 = bf16[128,72,128]{2,1,0:T(8,128)(2,1)S(1)} async-done(((bf16[128,72,128]{2,1,0:T(8,128)(2,1)}), bf16[128,72,128]{2,1,0:T(8,128)(2,1)S(1)}, u32[]{:S(2)}, u32[]{:S(2)}) %all-to-all-start.1) | async-done | bytes 2359328 | tf_op jit(solution)/shard_map/all_to_all | solution.py:662
  172.4 1.4 constant_dynamic-update-slice_fusion
  173.8 5.5 %all-to-all-start.2 = ((bf16[128,168,128]{2,1,0:T(8,128)(2,1)}), bf16[128,168,128]{2,1,0:T(8,128)(2,1)}, u32[]{:S(2)}, u32[]{:S(2)}) async-start(bf16[128,168,128]{2,1,0:T(8,128)(2,1)} %constant_dynamic-update-slice_fusion), calls=%async_computation.2 | async-start | bytes 11010048 | tf_op jit(solution)/shard_map/all_to_all | solution.py:662
  179.3 6.1 %shard_map.152 = bf16[1600,256]{1,0:T(8,128)(2,1)} custom-call(bf16[2304,256]{1,0:T(8,128)(2,1)} %bitcast.23, bf16[2160,256]{1,0:T(8,128)(2,1)} %get-tuple-element.58.hidden_ref), custom_call_target="tpu_custom_call" | custom-call | flops 2300000000 | bytes 5000000 | tf_op jit(solution)/shard_map/pallas_call | solution.py:532
  185.5 60.9 %all-to-all-done.2.back_ref = bf16[128,168,128]{2,1,0:T(8,128)(2,1)} async-done(((bf16[128,168,128]{2,1,0:T(8,128)(2,1)}), bf16[128,168,128]{2,1,0:T(8,128)(2,1)}, u32[]{:S(2)}, u32[]{:S(2)}) %all-to-all-start.2) | async-done | bytes 5505056 | tf_op jit(solution)/shard_map/all_to_all | solution.py:662
  246.4 1.4 slice.41.own_ref
  248.8 6.8 %shard_map.153 = (bf16[4,128,256]{2,1,0:T(8,128)(2,1)}, f32[4,64,128]{2,1,0:T(8,128)}) custom-call(s32[4]{0:T(128)} %first_ref.3, s32[4]{0:T(128)} %count_ref.3, s32[4]{0:T(128)} %live_ref.3, s32[128]{0:T(128)} %get-tuple-element.60.route_ref, bf16[4,128,256]{2,1,0:T(8,128)(2,1)} %feat_ref.3, f32[4,64,128]{2,1,0:T(8,128)} %weight_ref.3, ...), custom_call_target="tpu_custom_call" | custom-call | flops 600000000 | bytes 8000000 | tf_op jit(solution)/shard_map/pallas_call | solution.py:643
  256.6 4.1 %shard_map.154 = (f32[9,256,256]{2,1,0:T(8,128)}, f32[9,256,256]{2,1,0:T(8,128)}) custom-call(s32[2]{0:T(128)} %pad_add_fusion.spot_ref, bf16[128,40,128]{2,1,0:T(8,128)(2,1)} %copy-done, bf16[128,40,128]{2,1,0:T(8,128)(2,1)} %copy-done.1), custom_call_target="tpu_custom_call" | custom-call | flops 1000000 | bytes 7000000 | tf_op jit(solution)/shard_map/pallas_call | solution.py:571
  (31 shorter events, 9.6 us)
Async XLA Ops:
  12.9 12.3 %copy-start.2 = (bf16[4,1024,128]{2,1,0:T(8,128)(2,1)S(1)}, bf16[4,1024,128]{2,1,0:T(8,128)(2,1)}, u32[]{:S(2)}) copy-start(bf16[4,1024,128]{2,1,0:T(8,128)(2,1)} %get-tuple-element.38) | copy-start | bytes 3145732
  12.9 67.9 %all-to-all-start = ((bf16[128,136,128]{2,1,0:T(8,128)(2,1)}), bf16[128,136,128]{2,1,0:T(8,128)(2,1)}, u32[]{:S(2)}, u32[]{:S(2)}) async-start(bf16[128,136,128]{2,1,0:T(8,128)(2,1)} %get-tuple-element.37), calls=%async_computation | async-start | bytes 8912896 | tf_op jit(solution)/shard_map/all_to_all | solution.py:662
  92.0 4.8 %collective-permute-start = (bf16[160,256]{1,0:T(8,128)(2,1)}, bf16[160,256]{1,0:T(8,128)(2,1)S(1)}, u32[]{:S(2)}, u32[]{:S(2)}) collective-permute-start(bf16[160,256]{1,0:T(8,128)(2,1)} %get-tuple-element.50), channel_id=1, source_target_pairs={{0,1},{1,2},{2,3},{3,4},{4,5},{5,6},{6,7},{8,9},{9,10},{10,11},{11... | collective-permute-start | bytes 245768 | tf_op jit(solution)/shard_map/ppermute | solution.py:276
  94.8 6.0 %collective-permute-start.1 = (bf16[160,256]{1,0:T(8,128)(2,1)}, bf16[160,256]{1,0:T(8,128)(2,1)S(1)}, u32[]{:S(2)}, u32[]{:S(2)}) collective-permute-start(bf16[160,256]{1,0:T(8,128)(2,1)} %get-tuple-element.51), channel_id=1, source_target_pairs={{1,0},{2,1},{3,2},{4,3},{5,4},{6,5},{7,6},{9,8},{10,9},{11,10},{12... | collective-permute-start | bytes 245768 | tf_op jit(solution)/shard_map/ppermute | solution.py:276
  96.7 4.0 %copy-start.3 = (bf16[160,256]{1,0:T(8,128)(2,1)}, bf16[160,256]{1,0:T(8,128)(2,1)S(1)}, u32[]{:S(2)}) copy-start(bf16[160,256]{1,0:T(8,128)(2,1)S(1)} %collective-permute-done.left_ref) | copy-start | bytes 245764
  100.8 0.6 copy-start.4
  103.1 3.4 %collective-permute-start.2 = (bf16[192,256]{1,0:T(8,128)(2,1)}, bf16[192,256]{1,0:T(8,128)(2,1)S(1)}, u32[]{:S(2)}, u32[]{:S(2)}) collective-permute-start(bf16[192,256]{1,0:T(8,128)(2,1)} %get-tuple-element.52), channel_id=1, source_target_pairs={{0,8},{8,16},{16,24},{24,32},{32,40},{40,48},{48,56},{56,64},{64,7... | collective-permute-start | bytes 294920 | tf_op jit(solution)/shard_map/ppermute | solution.py:276
  104.4 5.6 %collective-permute-start.3 = (bf16[192,256]{1,0:T(8,128)(2,1)}, bf16[192,256]{1,0:T(8,128)(2,1)S(1)}, u32[]{:S(2)}, u32[]{:S(2)}) collective-permute-start(bf16[192,256]{1,0:T(8,128)(2,1)} %get-tuple-element.53), channel_id=1, source_target_pairs={{8,0},{16,8},{24,16},{32,24},{40,32},{48,40},{56,48},{64,56},{72,6... | collective-permute-start | bytes 294920 | tf_op jit(solution)/shard_map/ppermute | solution.py:276
  106.5 3.4 %copy-start.5 = (bf16[192,256]{1,0:T(8,128)(2,1)}, bf16[192,256]{1,0:T(8,128)(2,1)S(1)}, u32[]{:S(2)}) copy-start(bf16[192,256]{1,0:T(8,128)(2,1)S(1)} %collective-permute-done.2.above_ref) | copy-start | bytes 294916
  110.0 0.6 copy-start.6
  128.6 43.3 %all-to-all-start.1 = ((bf16[128,72,128]{2,1,0:T(8,128)(2,1)}), bf16[128,72,128]{2,1,0:T(8,128)(2,1)S(1)}, u32[]{:S(2)}, u32[]{:S(2)}) async-start(bf16[128,72,128]{2,1,0:T(8,128)(2,1)} %bitcast.19), calls=%async_computation.1 | async-start | bytes 4718592 | tf_op jit(solution)/shard_map/all_to_all | solution.py:662
  173.8 72.6 %all-to-all-start.2 = ((bf16[128,168,128]{2,1,0:T(8,128)(2,1)}), bf16[128,168,128]{2,1,0:T(8,128)(2,1)}, u32[]{:S(2)}, u32[]{:S(2)}) async-start(bf16[128,168,128]{2,1,0:T(8,128)(2,1)} %constant_dynamic-update-slice_fusion), calls=%async_computation.2 | async-start | bytes 11010048 | tf_op jit(solution)/shard_map/all_to_all | solution.py:662
  247.8 7.7 %copy-start = (bf16[128,40,128]{2,1,0:T(8,128)(2,1)}, bf16[128,40,128]{2,1,0:T(8,128)(2,1)S(1)}, u32[]{:S(2)}) copy-start(bf16[128,40,128]{2,1,0:T(8,128)(2,1)S(1)} %slice.41.own_ref) | copy-start | bytes 3932164
  247.8 7.7 %collective-permute-start.4 = (bf16[128,40,128]{2,1,0:T(8,128)(2,1)S(1)}, bf16[128,40,128]{2,1,0:T(8,128)(2,1)S(1)}, u32[]{:S(2)}, u32[]{:S(2)}) collective-permute-start(bf16[128,40,128]{2,1,0:T(8,128)(2,1)S(1)} %slice.41.own_ref), channel_id=1, source_target_pairs={{0,1},{1,0},{2,3},{3,2},{4,5},{5,4},{6,7},{7,6},{8,9},{9,8},{10,11... | collective-permute-start | bytes 3932168 | tf_op jit(solution)/shard_map/ppermute | solution.py:730
  255.6 1.1 copy-start.1
